TPU v7x, 512 devices: a whole 4x8x8 slice. The times are simulated.
512 devices in a mesh: pts: 512 (over x, y, z, core).
Axes of the slice: x: 4, y: 8, z: 8, core: 2. Of those that a mesh axis runs over, the one named last changes fastest.
Arguments:
- points: bfloat16 [262144, 256], P('pts'), may hold values from -24 to 24
- patch_ids: int32 [262144], P('pts'), may hold values from 0 to 639, never falling along the last dimension, each value on 1 to 512 neighbouring positions
- cell_ids: int32 [262144], P('pts'), may hold values from 0 to 65535, as said below
- norm_gain: float32 [256], replicated, may hold values from 0.8 to 2
- w_qkv: bfloat16 [256, 768], replicated, may hold values from -0.375 to 0.375
- w_out: bfloat16 [256, 256], replicated, may hold values from -0.375 to 0.375
- w_pool: bfloat16 [256, 512], replicated, may hold values from -0.375 to 0.375
- b_pool: float32 [512], replicated, may hold values from -4 to 4
- pool_gain: float32 [512], replicated, may hold values from 0.5 to 1.5
- cotangent: float32 [65536, 512], P('pts'), may hold values from -6 to 6
Outputs:
- grad_points: float32 [262144, 256], P('pts')
- grad_qkv: float32 [256, 768], replicated
- grad_w_out: float32 [256, 256], replicated
- grad_norm_gain: float32 [256], replicated
- grad_w_pool: float32 [256, 512], replicated
- grad_b_pool: float32 [512], replicated
- grad_pool_gain: float32 [512], replicated
Inputs may be any that keep to these rules, and one draw needn't show every extreme that they name: `patch_ids`: patch ids never fall; every patch has 1 to 512 points and some patch has exactly 512. `cell_ids`: cell ids never fall and every cell has a point; point 0 is in cell 0; points d * 512 to (d + 1) * 512 - 1 hold the first points of exactly the cells d * 128 to (d + 1) * 128 - 1, for d above 0 none of them among the first 128 points of that range, so for d above 0 those first points belong to cell d * 128 - 1.
All inputs are finite; a program needn't handle non-finite values.
Results may differ from a plain program's by a relative error of at most 0.024.
Values may be sent and summed in bfloat16 or wider, within the bound.
A program may use at most 64 MiB of HBM per device.

v0:
```python
import math

import jax
import jax.numpy as jnp
from jax import lax
from jax.sharding import PartitionSpec as P

HEADS = 16
PATCH = 512
QBLOCK = 512


EPS = 1e-05
ROOT_HALF = 0.7071067811865476
ROOT_TWO_PI = 2.5066282746310002


def padded(block, sides, width):
    for axis, dim in sides:
        count = lax.axis_size(axis)
        forward = [(i, i + 1) for i in range(count - 1)]
        backward = [(target, source) for source, target in forward]
        low = lax.ppermute(
            lax.slice_in_dim(block, block.shape[dim] - width, None, axis=dim), axis, forward
        )
        high = lax.ppermute(lax.slice_in_dim(block, 0, width, axis=dim), axis, backward)
        block = jnp.concatenate([low, block, high], axis=dim)
    return block


def from_behind(value, axis, steps):
    count = lax.axis_size(axis)
    initial, last = (max(0, -steps), min(count, count - steps))
    return lax.ppermute(value, axis, [(source, source + steps) for source in range(initial, last)])


def layer_stats(values):
    centered = values - jnp.mean(values, axis=-1, keepdims=True)
    inv_std = lax.rsqrt(jnp.mean(centered * centered, axis=-1, keepdims=True) + EPS)
    return (centered * inv_std, inv_std)


def norm_back(grad_normed, normed, inv_std):
    first_mean = jnp.mean(grad_normed, axis=-1, keepdims=True)
    second_mean = jnp.mean(grad_normed * normed, axis=-1, keepdims=True)
    return inv_std * (grad_normed - first_mean - normed * second_mean)


def gelu_slope(scaled):
    normal_cdf = 0.5 * (1.0 + jax.scipy.special.erf(scaled * ROOT_HALF))
    return normal_cdf + scaled * jnp.exp(-0.5 * scaled * scaled) / ROOT_TWO_PI


def inner_rows(left, right):
    return lax.dot_general(
        left, right, (((0,), (0,)), ((), ())), preferred_element_type=jnp.float32
    )


def against_rows(left, right):
    return lax.dot_general(
        left, right, (((1,), (1,)), ((), ())), preferred_element_type=jnp.float32
    )


def pool_rows(sums, counts, w_pool, b_pool, pool_gain, cotangent):
    pooled_mean = (sums / counts[:, None]).astype(jnp.bfloat16)
    pre_norm = jnp.dot(pooled_mean, w_pool, preferred_element_type=jnp.float32) + b_pool
    pooled_normed, pooled_inv = layer_stats(pre_norm)
    slope_grad = cotangent * gelu_slope(pooled_normed * pool_gain)
    grad_pre = norm_back(slope_grad * pool_gain, pooled_normed, pooled_inv)
    grad_pre_b = grad_pre.astype(jnp.bfloat16)
    share = against_rows(grad_pre_b, w_pool) / counts[:, None]
    return (pooled_mean, pooled_normed, slope_grad, grad_pre, grad_pre_b, share)


def body(
    points, patch_ids, cell_ids, norm_gain, w_qkv, w_out, w_pool, b_pool, pool_gain, cotangent
):
    row_count, feat_width = points.shape
    cell_count = cotangent.shape[0]
    head_size = feat_width // HEADS
    grouped = 2
    lane_count = grouped * head_size
    score_scale = 1.0 / math.sqrt(head_size)
    rim_width = PATCH
    key_window = QBLOCK + 2 * rim_width
    block_count = row_count // QBLOCK
    turn_count = HEADS // grouped * block_count
    feats = points.astype(jnp.float32)
    normed, inv_std = layer_stats(feats)
    hidden = (normed * norm_gain).astype(jnp.bfloat16)
    qkv = jnp.dot(hidden, w_qkv, preferred_element_type=jnp.float32).astype(jnp.bfloat16)
    queries = qkv[:, :feat_width]
    key_values = qkv[:, feat_width:]
    patch_marks = patch_ids + 1
    marks_ext = padded(patch_marks, (("pts", 0),), rim_width)
    kv_ext = padded(key_values, (("pts", 0),), rim_width)

    def tiles(turn):
        group = turn // block_count
        start = turn % block_count * QBLOCK
        column = group * lane_count
        q_tile = lax.dynamic_slice(queries, (start, column), (QBLOCK, lane_count)).reshape(
            QBLOCK, grouped, head_size
        )
        k_tile = lax.dynamic_slice(kv_ext, (start, column), (key_window, lane_count)).reshape(
            key_window, grouped, head_size
        )
        v_tile = lax.dynamic_slice(
            kv_ext, (start, feat_width + column), (key_window, lane_count)
        ).reshape(key_window, grouped, head_size)
        visible = (patch_marks[:, None] == marks_ext[None, :])[None]
        scores = (
            jnp.einsum("qgd,kgd->gqk", q_tile, k_tile, preferred_element_type=jnp.float32)
            * score_scale
        )
        return (group, start, column, q_tile, k_tile, v_tile, visible, scores)

    def forward_turn(turn, carry):
        attended_acc, totals_acc = carry
        group, start, column, q_tile, k_tile, v_tile, visible, scores = tiles(turn)
        masked = jnp.where(visible, scores, -jnp.inf)
        row_top = jnp.max(masked, axis=-1, keepdims=True)
        log_totals = row_top + jnp.log(jnp.sum(jnp.exp(masked - row_top), axis=-1, keepdims=True))
        weights = jnp.where(visible, jnp.exp(scores - log_totals), 0.0).astype(jnp.bfloat16)
        mixed_heads = jnp.einsum(
            "gqk,kgd->qgd", weights, v_tile, preferred_element_type=jnp.float32
        ).reshape(QBLOCK, lane_count)
        attended_acc = lax.dynamic_update_slice(attended_acc, mixed_heads, (start, column))
        totals_acc = lax.dynamic_update_slice(
            totals_acc, log_totals[:, :, 0], (group * grouped, start)
        )
        return (attended_acc, totals_acc)

    attended_full, log_totals = lax.fori_loop(
        0,
        turn_count,
        forward_turn,
        (
            jnp.zeros((row_count, feat_width), jnp.float32),
            jnp.zeros((HEADS, row_count), jnp.float32),
        ),
    )
    attended = attended_full.astype(jnp.bfloat16)
    mixed = (feats + jnp.dot(attended, w_out, preferred_element_type=jnp.float32)).astype(
        jnp.bfloat16
    )
    local_cells = cell_ids - lax.axis_index("pts") * cell_count
    slots = jnp.arange(cell_count, dtype=jnp.int32)
    member = slots[:, None] == local_cells[None, :]
    sums = jnp.dot(member.astype(jnp.bfloat16), mixed, preferred_element_type=jnp.float32)
    counts = jnp.sum(member.astype(jnp.float32), axis=1)
    leading = local_cells < 0
    lead_sum = jnp.dot(
        leading.astype(jnp.bfloat16)[None, :], mixed, preferred_element_type=jnp.float32
    )
    lead_count = jnp.sum(leading.astype(jnp.float32))
    lead_pack = jnp.concatenate(
        [lead_sum, jnp.full((1, feat_width), lead_count, jnp.float32)], axis=0
    )
    from_next = from_behind(lead_pack, "pts", -1)
    sums_all = sums.at[cell_count - 1].add(from_next[0])
    counts_all = counts.at[cell_count - 1].add(from_next[1, 0])
    pooled_mean, pooled_normed, slope_grad, grad_pre, grad_pre_b, share = pool_rows(
        sums_all, counts_all, w_pool, b_pool, pool_gain, cotangent
    )
    lead_share = from_behind(share[cell_count - 1 :], "pts", 1)[0]
    grad_w_pool = inner_rows(pooled_mean, grad_pre_b)
    grad_b_pool = jnp.sum(grad_pre, axis=0)
    grad_pool_gain = jnp.sum(slope_grad * pooled_normed, axis=0)
    dmixed = jnp.where(
        leading[:, None], lead_share[None, :], jnp.take(share, jnp.maximum(local_cells, 0), axis=0)
    )
    dmixed_b = dmixed.astype(jnp.bfloat16)
    grad_w_out = inner_rows(attended, dmixed_b)
    grad_scale = 1.0 / math.sqrt(row_count * lax.axis_size("pts"))
    dattended = against_rows(dmixed_b, w_out).astype(jnp.bfloat16)
    deltas = jnp.sum(
        (dattended.astype(jnp.float32) * attended_full).reshape(row_count, HEADS, head_size),
        axis=-1,
    ).T

    def backward_turn(turn, carry):
        dquery_acc, dkv_acc = carry
        group, start, column, q_tile, k_tile, v_tile, visible, scores = tiles(turn)
        totals_tile = lax.dynamic_slice(log_totals, (group * grouped, start), (grouped, QBLOCK))
        delta_tile = lax.dynamic_slice(deltas, (group * grouped, start), (grouped, QBLOCK))
        dout_tile = lax.dynamic_slice(dattended, (start, column), (QBLOCK, lane_count)).reshape(
            QBLOCK, grouped, head_size
        )
        weights = jnp.where(visible, jnp.exp(scores - totals_tile[:, :, None]), 0.0)
        weights_b = weights.astype(jnp.bfloat16)
        dweights = jnp.einsum("qgd,kgd->gqk", dout_tile, v_tile, preferred_element_type=jnp.float32)
        dscores = (weights * (dweights - delta_tile[:, :, None]) * score_scale).astype(jnp.bfloat16)
        dq_tile = jnp.einsum(
            "gqk,kgd->qgd", dscores, k_tile, preferred_element_type=jnp.float32
        ).reshape(QBLOCK, lane_count)
        dk_tile = jnp.einsum(
            "gqk,qgd->kgd", dscores, q_tile, preferred_element_type=jnp.float32
        ).reshape(key_window, lane_count)
        dv_tile = jnp.einsum(
            "gqk,qgd->kgd", weights_b, dout_tile, preferred_element_type=jnp.float32
        ).reshape(key_window, lane_count)
        dquery_acc = lax.dynamic_update_slice(dquery_acc, dq_tile, (start, column))
        old_keys = lax.dynamic_slice(dkv_acc, (start, column), (key_window, lane_count))
        dkv_acc = lax.dynamic_update_slice(dkv_acc, old_keys + dk_tile, (start, column))
        old_values = lax.dynamic_slice(
            dkv_acc, (start, feat_width + column), (key_window, lane_count)
        )
        dkv_acc = lax.dynamic_update_slice(
            dkv_acc, old_values + dv_tile, (start, feat_width + column)
        )
        return (dquery_acc, dkv_acc)

    dquery, dkv_ext = lax.fori_loop(
        0,
        turn_count,
        backward_turn,
        (
            jnp.zeros((row_count, feat_width), jnp.float32),
            jnp.zeros((row_count + 2 * rim_width, 2 * feat_width), jnp.float32),
        ),
    )
    rim_pack = jnp.concatenate([dkv_ext[:rim_width], dkv_ext[rim_width + row_count :]], axis=0)
    rim_back = padded(rim_pack.astype(jnp.bfloat16), (("pts", 0),), rim_width).astype(
        rim_pack.dtype
    )
    from_prev = rim_back[:rim_width]
    from_next_rows = rim_back[3 * rim_width :]
    dkv_own = dkv_ext[rim_width : rim_width + row_count]
    dkv_own = dkv_own.at[:rim_width].add(from_prev)
    dkv_own = dkv_own.at[row_count - rim_width :].add(from_next_rows)
    dqkv = jnp.concatenate([dquery, dkv_own], axis=1).astype(jnp.bfloat16)
    grad_qkv = inner_rows(hidden, dqkv)
    dhidden = against_rows(dqkv, w_qkv)
    grad_norm_gain = jnp.sum(dhidden * normed, axis=0)
    grad_points = dmixed + norm_back(dhidden * norm_gain, normed, inv_std)
    every_sum = lax.psum(
        (grad_qkv, grad_norm_gain, grad_w_pool, grad_b_pool, grad_pool_gain, grad_w_out), "pts"
    )
    summed_qkv, summed_gain, summed_pool, summed_bias, summed_pgain, summed_out = every_sum
    return (
        grad_points,
        summed_qkv * grad_scale,
        summed_out * grad_scale,
        summed_gain * grad_scale,
        summed_pool * grad_scale,
        summed_bias * grad_scale,
        summed_pgain * grad_scale,
    )


def solution(mesh):
    in_specs = (P("pts", None), P("pts"), P("pts"), P(), P(), P(), P(), P(), P(), P("pts", None))
    out_specs = (P("pts", None), P(), P(), P(), P(), P(), P())
    return jax.shard_map(body, mesh=mesh, in_specs=in_specs, out_specs=out_specs, check_vma=False)
```

profile of v0, /device:TPU:1, one launch (start us, length us, event | category | flops | bytes accessed | tf_op | source)
XLA Modules:
  0.0 633.2 jit_solution(15471245297626052266)
XLA Ops:
  11.1 8.8 %collective-permute-start.1 = (bf16[512,512]{1,0:T(8,128)(2,1)S(1)}, bf16[512,512]{1,0:T(8,128)(2,1)S(1)}, u32[]{:S(2)}, u32[]{:S(2)}) collective-permute-start(bf16[512,512]{1,0:T(8,128)(2,1)S(1)} %slice.105), channel_id=1, source_target_pairs={{1,0},{2,1},{3,2},{4,3},{5,4},{6,5},{7,6},{8,7},{9,8},{10,9},{11,1... | collective-permute-start | bytes 1572872 | tf_op jit(solution)/shard_map/ppermute | solution.py:26
  19.9 1.9 collective-permute-start
  22.5 2.4 collective-permute-start.3
  24.9 3.1 collective-permute-start.2
  34.6 1.7 copy.23
  37.0 104.7 %while.40 = (s32[]{:T(128)}, f32[512,256]{0,1:T(8,128)S(1)}, f32[16,512]{1,0:T(8,128)}, bf16[1536,512]{0,1:T(8,128)(2,1)S(1)}, s32[512]{0:T(512)S(1)}, /*index=5...) while((s32[]{:T(128)}, f32[512,256]{0,1:T(8,128)S(1)}, ...), condition=%wide.region_5.6_spmd, body=%wide.region_2.5_spmd.sunk | while | flops 118750216 | bytes 48505204 | solution.py:136
  39.0 4.9 select_reduce_fusion.2
  43.9 3.9 exponential_reduce_fusion.2
  52.1 4.9 select_reduce_fusion.2
  57.0 3.9 exponential_reduce_fusion.2
  65.2 4.9 select_reduce_fusion.2
  70.1 3.9 exponential_reduce_fusion.2
  78.3 4.9 select_reduce_fusion.2
  83.2 3.9 exponential_reduce_fusion.2
  91.4 4.9 select_reduce_fusion.2
  96.3 3.9 exponential_reduce_fusion.2
  104.5 4.9 select_reduce_fusion.2
  109.4 3.9 exponential_reduce_fusion.2
  117.6 4.9 select_reduce_fusion.2
  122.5 3.9 exponential_reduce_fusion.2
  130.6 4.9 select_reduce_fusion.2
  135.6 3.9 exponential_reduce_fusion.2
  144.6 1.9 collective-permute-start.4
  147.4 2.1 collective-permute-done.4
  150.1 2.1 fusion.42
  153.6 1.9 multiply_reduce_fusion.1
  158.1 2.1 collective-permute-start.5
  161.5 1.7 gather_fusion
  163.3 2.5 bitcast_reduce_fusion
  166.1 146.4 %while.41 = (s32[]{:T(128)}, bf16[512,256]{0,1:T(8,128)(2,1)}, f32[1536,512]{0,1:T(8,128)S(1)}, bf16[1536,512]{0,1:T(8,128)(2,1)}, s32[512]{0:T(512)S(1)}, /*ind...) while((s32[]{:T(128)}, bf16[512,256]{0,1:T(8,128)(2,1)}, ...), condition=%wide.region_14.15_spmd, body=%wide.region_13.14_spmd.sunk | while | flops 269844480 | bytes 52990464 | solution.py:216
  169.2 4.6 fusion.112
  175.0 5.4 multiply_convert_fusion.2
  182.7 1.7 fusion.115
  187.4 4.6 fusion.112
  193.3 5.4 multiply_convert_fusion.2
  200.9 1.7 fusion.115
  205.7 4.6 fusion.112
  211.6 5.4 multiply_convert_fusion.2
  219.2 1.7 fusion.115
  224.0 4.6 fusion.112
  229.9 5.4 multiply_convert_fusion.2
  237.5 1.7 fusion.115
  242.3 4.6 fusion.112
  248.2 5.5 multiply_convert_fusion.2
  255.8 1.7 fusion.115
  260.6 4.6 fusion.112
  266.5 5.4 multiply_convert_fusion.2
  274.1 1.7 fusion.115
  278.9 4.6 fusion.112
  284.8 5.4 multiply_convert_fusion.2
  292.4 1.7 fusion.115
  297.2 4.6 fusion.112
  303.1 5.4 multiply_convert_fusion.2
  310.7 1.7 fusion.115
  312.9 2.9 collective-permute-start.7
  315.8 2.8 collective-permute-start.6
  319.7 1.8 fusion.35
  321.5 2.0 collective-permute-done.7
  327.2 120.2 %all-reduce.1 = (f32[256]{0:T(256)S(1)}, f32[512]{0:T(512)S(1)}, f32[512]{0:T(512)S(1)}) all-reduce(f32[256]{0:T(256)S(1)} %get-tuple-element.535, f32[512]{0:T(512)S(1)} %copy-done.32, f32[512]{0:T(512)S(1)} %copy-done.31), channel_id=1, replica_groups=mesh['pts'=512] {'pts'}, use_global_device_ids=true, to_apply=%region_20.21 | all-reduce | flops 1280 | bytes 10240 | tf_op jit(solution)/shard_map/psum | solution.py:239
  449.1 1.9 fusion.23
  451.1 169.7 %all-reduce.5.cloned.1.call-done = (f32[256,768]{1,0:T(8,128)}, f32[256,256]{1,0:T(8,128)}, f32[256,512]{1,0:T(8,128)}) async-done(((f32[256,768]{1,0:T(8,128)}, f32[256,256]{1,0:T(8,128)}, f32[256,512]{1,0:T(8,128)}), (f32[256,768]{1,0:T(8,128)}, f32[256,256]{1,0:T(8,128)}, f32[256,512]{1,0:T(8,128)})) %all-reduce.5.cloned.1.call-update) | async-done | bytes 1572880 | tf_op jit(solution)/shard_map/psum | solution.py:239
  620.7 2.1 broadcast_multiply_fusion
  622.8 1.7 broadcast_multiply_fusion.2
  624.5 1.9 broadcast_multiply_fusion.1
  (373 shorter events, 113.3 us)
Async XLA Ops:
  7.2 613.5 %all-reduce.5.cloned.1.call-start = ((), (), s32[]{:S(2)}) async-start(), calls=%async_computation | async-start | bytes 3145728 | tf_op jit(solution)/shard_map/psum | solution.py:239
  8.4 14.1 %copy-start.23 = (f32[512]{0:T(512)}, f32[512]{0:T(512)S(1)}, u32[]{:S(2)}) copy-start(f32[512]{0:T(512)S(1)} %broadcast_multiply_fusion.7) | copy-start | bytes 6148
  9.6 15.3 %copy-start.25 = (f32[512]{0:T(512)}, f32[512]{0:T(512)S(1)}, u32[]{:S(2)}) copy-start(f32[512]{0:T(512)S(1)} %add_rsqrt_fusion) | copy-start | bytes 6148
  11.1 22.2 %collective-permute-start.1 = (bf16[512,512]{1,0:T(8,128)(2,1)S(1)}, bf16[512,512]{1,0:T(8,128)(2,1)S(1)}, u32[]{:S(2)}, u32[]{:S(2)}) collective-permute-start(bf16[512,512]{1,0:T(8,128)(2,1)S(1)} %slice.105), channel_id=1, source_target_pairs={{1,0},{2,1},{3,2},{4,3},{5,4},{6,5},{7,6},{8,7},{9,8},{10,9},{11,1... | collective-permute-start | bytes 1572872 | tf_op jit(solution)/shard_map/ppermute | solution.py:26
  19.9 13.5 %collective-permute-start = (bf16[512,512]{1,0:T(8,128)(2,1)S(1)}, bf16[512,512]{1,0:T(8,128)(2,1)S(1)}, u32[]{:S(2)}, u32[]{:S(2)}) collective-permute-start(bf16[512,512]{1,0:T(8,128)(2,1)S(1)} %slice.105), channel_id=1, source_target_pairs={{0,1},{1,2},{2,3},{3,4},{4,5},{5,6},{6,7},{7,8},{8,9},{9,10},{10,1... | collective-permute-start | bytes 1572872 | tf_op jit(solution)/shard_map/ppermute | solution.py:23
  22.5 10.8 %collective-permute-start.3 = (s32[512]{0:T(512)S(1)}, s32[512]{0:T(512)S(1)}, u32[]{:S(2)}, u32[]{:S(2)}) collective-permute-start(s32[512]{0:T(512)S(1)} %broadcast_add_fusion), channel_id=1, source_target_pairs={{1,0},{2,1},{3,2},{4,3},{5,4},{6,5},{7,6},{8,7},{9,8},{10,9},{11,1... | collective-permute-start | bytes 6152 | tf_op jit(solution)/shard_map/ppermute | solution.py:26
  24.9 8.4 %collective-permute-start.2 = (s32[512]{0:T(512)S(1)}, s32[512]{0:T(512)S(1)}, u32[]{:S(2)}, u32[]{:S(2)}) collective-permute-start(s32[512]{0:T(512)S(1)} %broadcast_add_fusion), channel_id=1, source_target_pairs={{0,1},{1,2},{2,3},{3,4},{4,5},{5,6},{6,7},{7,8},{8,9},{9,10},{10,1... | collective-permute-start | bytes 6152 | tf_op jit(solution)/shard_map/ppermute | solution.py:23
  37.0 104.8 %copy-start.11 = (bf16[512,256]{1,0:T(8,128)(2,1)S(1)}, bf16[512,256]{1,0:T(8,128)(2,1)}, u32[]{:S(2)}) copy-start(bf16[512,256]{1,0:T(8,128)(2,1)} %param.26) | copy-start | bytes 786436
  43.9 4.6 copy-start.14
  57.0 4.6 copy-start.14
  70.1 4.6 copy-start.14
  83.2 4.6 copy-start.14
  96.3 4.6 copy-start.14
  122.5 4.6 copy-start.14
  141.7 21.4 %copy-start.8 = (bf16[1536,512]{0,1:T(8,128)(2,1)}, bf16[1536,512]{0,1:T(8,128)(2,1)S(1)}, u32[]{:S(2)}) copy-start(bf16[1536,512]{0,1:T(8,128)(2,1)S(1)} %get-tuple-element.844) | copy-start | bytes 4718596
  141.8 21.5 %copy-start.6 = (f32[512,256]{0,1:T(8,128)}, f32[512,256]{0,1:T(8,128)S(1)}, u32[]{:S(2)}) copy-start(f32[512,256]{0,1:T(8,128)S(1)} %get-tuple-element.497) | copy-start | bytes 1572868
  141.8 13.8 %copy-start.30 = (f32[512]{0:T(512)S(1)}, f32[512]{0:T(512)}, u32[]{:S(2)}) copy-start(f32[512]{0:T(512)} %param.34) | copy-start | bytes 6148
  144.6 4.9 collective-permute-start.4
  149.5 13.7 %copy-start.16 = (f32[128,256]{1,0:T(8,128)}, f32[128,256]{1,0:T(8,128)S(1)}, u32[]{:S(2)}) copy-start(f32[128,256]{1,0:T(8,128)S(1)} %scatter-add.6) | copy-start | bytes 393220
  155.5 7.7 %copy-start.18 = (bf16[256,256]{1,0:T(8,128)(2,1)S(1)}, bf16[256,256]{1,0:T(8,128)(2,1)}, u32[]{:S(2)}) copy-start(bf16[256,256]{1,0:T(8,128)(2,1)} %param.31) | copy-start | bytes 393220
  155.5 7.7 %copy-start.28 = (pred[512]{0:T(512)(128)(4,1)S(1)}, pred[512]{0:T(512)(128)(4,1)}, u32[]{:S(2)}) copy-start(pred[512]{0:T(512)(128)(4,1)} %copy-done.27) | copy-start | bytes 1540
  156.3 9.4 %copy-start.19 = (bf16[128,512]{1,0:T(8,128)(2,1)}, bf16[128,512]{1,0:T(8,128)(2,1)S(1)}, u32[]{:S(2)}) copy-start(bf16[128,512]{1,0:T(8,128)(2,1)S(1)} %get-tuple-element.584) | copy-start | bytes 393220
  158.1 5.2 collective-permute-start.5
  174.5 8.1 %slice-start = ((s8[6291456]{0:T(1024)(128)(4,1)}), s8[4194304]{0:T(1024)(128)(4,1)S(1)}, s32[]{:S(2)}) async-start(s8[6291456]{0:T(1024)(128)(4,1)} %bitcast.95), calls=%async_computation.1 | async-start | bytes 8388608 | tf_op jit(solution)/shard_map/while
  175.0 5.5 copy-start.2
  175.0 7.6 %slice-start.1 = ((s8[6291456]{0:T(1024)(128)(4,1)}), s8[2097152]{0:T(1024)(128)(4,1)S(1)}, s32[]{:S(2)}) async-start(s8[6291456]{0:T(1024)(128)(4,1)} %bitcast.95), calls=%async_computation.2 | async-start | bytes 4194304 | tf_op jit(solution)/shard_map/while
  192.8 8.1 %slice-start = ((s8[6291456]{0:T(1024)(128)(4,1)}), s8[4194304]{0:T(1024)(128)(4,1)S(1)}, s32[]{:S(2)}) async-start(s8[6291456]{0:T(1024)(128)(4,1)} %bitcast.95), calls=%async_computation.1 | async-start | bytes 8388608 | tf_op jit(solution)/shard_map/while
  193.3 5.5 copy-start.2
  193.3 7.6 %slice-start.1 = ((s8[6291456]{0:T(1024)(128)(4,1)}), s8[2097152]{0:T(1024)(128)(4,1)S(1)}, s32[]{:S(2)}) async-start(s8[6291456]{0:T(1024)(128)(4,1)} %bitcast.95), calls=%async_computation.2 | async-start | bytes 4194304 | tf_op jit(solution)/shard_map/while
  211.1 8.1 %slice-start = ((s8[6291456]{0:T(1024)(128)(4,1)}), s8[4194304]{0:T(1024)(128)(4,1)S(1)}, s32[]{:S(2)}) async-start(s8[6291456]{0:T(1024)(128)(4,1)} %bitcast.95), calls=%async_computation.1 | async-start | bytes 8388608 | tf_op jit(solution)/shard_map/while
  211.6 5.5 copy-start.2
  211.6 7.6 %slice-start.1 = ((s8[6291456]{0:T(1024)(128)(4,1)}), s8[2097152]{0:T(1024)(128)(4,1)S(1)}, s32[]{:S(2)}) async-start(s8[6291456]{0:T(1024)(128)(4,1)} %bitcast.95), calls=%async_computation.2 | async-start | bytes 4194304 | tf_op jit(solution)/shard_map/while
  229.4 8.1 %slice-start = ((s8[6291456]{0:T(1024)(128)(4,1)}), s8[4194304]{0:T(1024)(128)(4,1)S(1)}, s32[]{:S(2)}) async-start(s8[6291456]{0:T(1024)(128)(4,1)} %bitcast.95), calls=%async_computation.1 | async-start | bytes 8388608 | tf_op jit(solution)/shard_map/while
  229.9 5.5 copy-start.2
  229.9 7.6 %slice-start.1 = ((s8[6291456]{0:T(1024)(128)(4,1)}), s8[2097152]{0:T(1024)(128)(4,1)S(1)}, s32[]{:S(2)}) async-start(s8[6291456]{0:T(1024)(128)(4,1)} %bitcast.95), calls=%async_computation.2 | async-start | bytes 4194304 | tf_op jit(solution)/shard_map/while
  247.7 8.1 %slice-start = ((s8[6291456]{0:T(1024)(128)(4,1)}), s8[4194304]{0:T(1024)(128)(4,1)S(1)}, s32[]{:S(2)}) async-start(s8[6291456]{0:T(1024)(128)(4,1)} %bitcast.95), calls=%async_computation.1 | async-start | bytes 8388608 | tf_op jit(solution)/shard_map/while
  248.2 5.5 copy-start.2
  248.2 7.6 %slice-start.1 = ((s8[6291456]{0:T(1024)(128)(4,1)}), s8[2097152]{0:T(1024)(128)(4,1)S(1)}, s32[]{:S(2)}) async-start(s8[6291456]{0:T(1024)(128)(4,1)} %bitcast.95), calls=%async_computation.2 | async-start | bytes 4194304 | tf_op jit(solution)/shard_map/while
  266.0 8.1 %slice-start = ((s8[6291456]{0:T(1024)(128)(4,1)}), s8[4194304]{0:T(1024)(128)(4,1)S(1)}, s32[]{:S(2)}) async-start(s8[6291456]{0:T(1024)(128)(4,1)} %bitcast.95), calls=%async_computation.1 | async-start | bytes 8388608 | tf_op jit(solution)/shard_map/while
  266.5 5.5 copy-start.2
  266.5 7.6 %slice-start.1 = ((s8[6291456]{0:T(1024)(128)(4,1)}), s8[2097152]{0:T(1024)(128)(4,1)S(1)}, s32[]{:S(2)}) async-start(s8[6291456]{0:T(1024)(128)(4,1)} %bitcast.95), calls=%async_computation.2 | async-start | bytes 4194304 | tf_op jit(solution)/shard_map/while
  284.2 8.1 %slice-start = ((s8[6291456]{0:T(1024)(128)(4,1)}), s8[4194304]{0:T(1024)(128)(4,1)S(1)}, s32[]{:S(2)}) async-start(s8[6291456]{0:T(1024)(128)(4,1)} %bitcast.95), calls=%async_computation.1 | async-start | bytes 8388608 | tf_op jit(solution)/shard_map/while
  284.8 5.5 copy-start.2
  284.8 7.6 %slice-start.1 = ((s8[6291456]{0:T(1024)(128)(4,1)}), s8[2097152]{0:T(1024)(128)(4,1)S(1)}, s32[]{:S(2)}) async-start(s8[6291456]{0:T(1024)(128)(4,1)} %bitcast.95), calls=%async_computation.2 | async-start | bytes 4194304 | tf_op jit(solution)/shard_map/while
  302.5 8.1 %slice-start = ((s8[6291456]{0:T(1024)(128)(4,1)}), s8[4194304]{0:T(1024)(128)(4,1)S(1)}, s32[]{:S(2)}) async-start(s8[6291456]{0:T(1024)(128)(4,1)} %bitcast.95), calls=%async_computation.1 | async-start | bytes 8388608 | tf_op jit(solution)/shard_map/while
  303.1 5.5 copy-start.2
  303.1 7.6 %slice-start.1 = ((s8[6291456]{0:T(1024)(128)(4,1)}), s8[2097152]{0:T(1024)(128)(4,1)S(1)}, s32[]{:S(2)}) async-start(s8[6291456]{0:T(1024)(128)(4,1)} %bitcast.95), calls=%async_computation.2 | async-start | bytes 4194304 | tf_op jit(solution)/shard_map/while
  312.5 6.1 copy-start.17
  312.5 6.1 copy-start.20
  312.5 6.1 copy-start.36
  312.5 7.2 %copy-start.4 = (f32[512,256]{1,0:T(8,128)S(1)}, f32[512,256]{1,0:T(8,128)}, u32[]{:S(2)}) copy-start(f32[512,256]{1,0:T(8,128)} %copy-done.3) | copy-start | bytes 1572868
  312.5 7.2 %copy-start.7 = (f32[512,256]{0,1:T(8,128)S(1)}, f32[512,256]{0,1:T(8,128)}, u32[]{:S(2)}) copy-start(f32[512,256]{0,1:T(8,128)} %copy-done.6) | copy-start | bytes 1572868
  312.5 7.2 %copy-start.29 = (pred[512]{0:T(512)(128)(4,1)S(1)}, pred[512]{0:T(512)(128)(4,1)}, u32[]{:S(2)}) copy-start(pred[512]{0:T(512)(128)(4,1)} %copy-done.27) | copy-start | bytes 1540
  312.5 7.2 %copy-start.33 = (pred[512]{0:T(512)(128)(4,1)S(1)}, pred[512]{0:T(512)(128)(4,1)}, u32[]{:S(2)}) copy-start(pred[512]{0:T(512)(128)(4,1)} %get-tuple-element.585) | copy-start | bytes 1540
  312.8 12.1 %copy-start.12 = (bf16[512,256]{1,0:T(8,128)(2,1)S(1)}, bf16[512,256]{1,0:T(8,128)(2,1)}, u32[]{:S(2)}) copy-start(bf16[512,256]{1,0:T(8,128)(2,1)} %param.26) | copy-start | bytes 786436
  312.8 12.1 %copy-start.21 = (bf16[512,256]{0,1:T(8,128)(2,1)S(1)}, bf16[512,256]{0,1:T(8,128)(2,1)}, u32[]{:S(2)}) copy-start(bf16[512,256]{0,1:T(8,128)(2,1)} %get-tuple-element.499) | copy-start | bytes 786436
  312.8 12.1 %copy-start.24 = (f32[512]{0:T(512)S(1)}, f32[512]{0:T(512)}, u32[]{:S(2)}) copy-start(f32[512]{0:T(512)} %copy-done.23) | copy-start | bytes 6148
  312.8 12.1 %copy-start.26 = (f32[512]{0:T(512)S(1)}, f32[512]{0:T(512)}, u32[]{:S(2)}) copy-start(f32[512]{0:T(512)} %copy-done.25) | copy-start | bytes 6148
  312.8 12.1 %copy-start.34 = (f32[256]{0:T(256)S(1)}, f32[256]{0:T(256)}, u32[]{:S(2)}) copy-start(f32[256]{0:T(256)} %param.29) | copy-start | bytes 3076
  312.9 10.6 %collective-permute-start.7 = (bf16[512,512]{0,1:T(8,128)(2,1)S(1)}, bf16[512,512]{0,1:T(8,128)(2,1)S(1)}, u32[]{:S(2)}, u32[]{:S(2)}) collective-permute-start(bf16[512,512]{0,1:T(8,128)(2,1)S(1)} %get-tuple-element.601), channel_id=1, source_target_pairs={{1,0},{2,1},{3,2},{4,3},{5,4},{6,5},{7,6},{8,7},{9,8},{10,9},{11,1... | collective-permute-start | bytes 1572872 | tf_op jit(solution)/shard_map/ppermute | solution.py:26
  315.8 8.9 %collective-permute-start.6 = (bf16[512,512]{0,1:T(8,128)(2,1)S(1)}, bf16[512,512]{0,1:T(8,128)(2,1)S(1)}, u32[]{:S(2)}, u32[]{:S(2)}) collective-permute-start(bf16[512,512]{0,1:T(8,128)(2,1)S(1)} %get-tuple-element.600), channel_id=1, source_target_pairs={{0,1},{1,2},{2,3},{3,4},{4,5},{5,6},{6,7},{7,8},{8,9},{9,10},{10,1... | collective-permute-start | bytes 1572872 | tf_op jit(solution)/shard_map/ppermute | solution.py:23
  325.0 124.2 %copy-start.5 = (f32[512,256]{1,0:T(8,128)S(1)}, f32[512,256]{1,0:T(8,128)}, u32[]{:S(2)}) copy-start(f32[512,256]{1,0:T(8,128)} %copy-done.3) | copy-start | bytes 1572868
  325.0 124.1 %copy-start.13 = (bf16[512,256]{1,0:T(8,128)(2,1)S(1)}, bf16[512,256]{1,0:T(8,128)(2,1)}, u32[]{:S(2)}) copy-start(bf16[512,256]{1,0:T(8,128)(2,1)} %param.26) | copy-start | bytes 786436
  325.0 124.1 %copy-start.35 = (f32[256]{0:T(256)S(1)}, f32[256]{0:T(256)}, u32[]{:S(2)}) copy-start(f32[256]{0:T(256)} %param.29) | copy-start | bytes 3076
  (40 other events, 127.6 us)
Sparse Core Ops, SparseCore 0:
  327.3 293.3 all-reduce.4
where the time goes:
time: 637 us; the launch traced here: 633 us
  waiting for transfers between devices  175 us (27%)
  matrix products  171 us (27%)
  blocking collectives  120 us (19%)
  other arithmetic  68.8 us (11%)
  local copies, waits for them, and re-layouts  55.9 us (9%)
  starting transfers between devices  26 us (4%)
  between operations  14.7 us (2%)
    psum x1, waiting for transfers between devices, body(): lax.psum((grad_qkv, grad_norm_gain, grad_w_pool, grad_b_pool, grad_pool_g...  170 us
    psum x1, blocking collectives, body(): lax.psum((grad_qkv, grad_norm_gain, grad_w_pool, grad_b_pool, grad_pool_g...  120 us
    dot_general x16, matrix products, tiles(): jnp.einsum('qgd,kgd->gqk', q_tile, k_tile, preferred_element_type=jnp.flo...  76.1 us
    dot_general x8, matrix products, backward_turn(): jnp.einsum('qgd,kgd->gqk', dout_tile, v_tile, preferred_element_type=jnp....  43.6 us
    reduce_sum x8, other arithmetic, forward_turn(): jnp.sum(jnp.exp(masked - row_top), axis=-1, keepdims=True)  31.4 us
    ppermute x3, starting transfers between devices, padded(): lax.ppermute(lax.slice_in_dim(block, 0, width, axis=dim), axis, backward)  14.1 us
    dot_general x8, matrix products, backward_turn(): jnp.einsum('gqk,qgd->kgd', weights_b, dout_tile, preferred_element_type=j...  13.5 us
    dynamic_slice x8, local copies, waits for them, and re-layouts, tiles(): lax.dynamic_slice(kv_ext, (start, feat_width + column), (key_window, lane...  13.1 us
  transfers between devices with their start and end apart: 9, of which 4 were waited for; matrix products, arithmetic and copies ran while one was open for 3% of the time, Pallas kernels for 0%

commit v1 on v0

v1 whole, which is shorter than its diff:
```python
import functools
import math

import jax
import jax.numpy as jnp
from jax import lax
from jax.experimental import pallas as pl
from jax.experimental.pallas import tpu as pltpu
from jax.sharding import PartitionSpec as P

PATCH = 512


EPS = 1e-05
ROOT_HALF = 0.7071067811865476
ROOT_TWO_PI = 2.5066282746310002


def padded(block, sides, width):
    for axis, dim in sides:
        count = lax.axis_size(axis)
        forward = [(i, i + 1) for i in range(count - 1)]
        backward = [(target, source) for source, target in forward]
        low = lax.ppermute(
            lax.slice_in_dim(block, block.shape[dim] - width, None, axis=dim), axis, forward
        )
        high = lax.ppermute(lax.slice_in_dim(block, 0, width, axis=dim), axis, backward)
        block = jnp.concatenate([low, block, high], axis=dim)
    return block


def from_behind(value, axis, steps):
    count = lax.axis_size(axis)
    initial, last = (max(0, -steps), min(count, count - steps))
    return lax.ppermute(value, axis, [(source, source + steps) for source in range(initial, last)])


def layer_stats(values):
    centered = values - jnp.mean(values, axis=-1, keepdims=True)
    inv_std = lax.rsqrt(jnp.mean(centered * centered, axis=-1, keepdims=True) + EPS)
    return (centered * inv_std, inv_std)


def norm_back(grad_normed, normed, inv_std):
    first_mean = jnp.mean(grad_normed, axis=-1, keepdims=True)
    second_mean = jnp.mean(grad_normed * normed, axis=-1, keepdims=True)
    return inv_std * (grad_normed - first_mean - normed * second_mean)


def gelu_slope(scaled):
    normal_cdf = 0.5 * (1.0 + jax.scipy.special.erf(scaled * ROOT_HALF))
    return normal_cdf + scaled * jnp.exp(-0.5 * scaled * scaled) / ROOT_TWO_PI


def inner_rows(left, right):
    return lax.dot_general(
        left, right, (((0,), (0,)), ((), ())), preferred_element_type=jnp.float32
    )


def against_rows(left, right):
    return lax.dot_general(
        left, right, (((1,), (1,)), ((), ())), preferred_element_type=jnp.float32
    )


def pool_rows(sums, counts, w_pool, b_pool, pool_gain, cotangent):
    pooled_mean = (sums / counts[:, None]).astype(jnp.bfloat16)
    pre_norm = jnp.dot(pooled_mean, w_pool, preferred_element_type=jnp.float32) + b_pool
    pooled_normed, pooled_inv = layer_stats(pre_norm)
    slope_grad = cotangent * gelu_slope(pooled_normed * pool_gain)
    grad_pre = norm_back(slope_grad * pool_gain, pooled_normed, pooled_inv)
    grad_pre_b = grad_pre.astype(jnp.bfloat16)
    share = against_rows(grad_pre_b, w_pool) / counts[:, None]
    return (pooled_mean, pooled_normed, slope_grad, grad_pre, grad_pre_b, share)


HALF = 128
PER_HALF = 8
HEAD_SIZE = 16
TILE = 256
CHUNK = 256
WINDOW = 3 * PATCH
FAR = float(2**30)
DIGIT = 32
LOG_LANE = 64


def head_lanes(h):
    lane = lax.broadcasted_iota(jnp.int32, (1, 2 * HALF), 1)
    own = (lane >= h * HEAD_SIZE) & (lane < (h + 1) * HEAD_SIZE)
    marks = (lane >= HALF) & (lane < HALF + LOG_LANE)
    terms = (lane >= HALF + LOG_LANE) & (lane < HALF + LOG_LANE + 24) & (lane % PER_HALF == h)
    return (own | marks | terms).astype(jnp.float32).astype(jnp.bfloat16)


def three_terms(columns):
    lane = lax.broadcasted_iota(jnp.int32, (1, HALF), 1)
    placed = jnp.zeros((columns[0].shape[0], HALF), jnp.float32)
    for h, column in enumerate(columns):
        here = (lane >= LOG_LANE) & (lane < LOG_LANE + 24) & (lane % PER_HALF == h)
        placed = jnp.where(here, column, placed)
    first = placed.astype(jnp.bfloat16).astype(jnp.float32)
    second = (placed - first).astype(jnp.bfloat16).astype(jnp.float32)
    third = placed - first - second
    which = (lane - LOG_LANE) // PER_HALF
    return jnp.where(which == 0, first, jnp.where(which == 1, second, third))


def forward_kernel(spans, q_ref, f_ref, kg_ref, v_ref, att_ref, logs_ref, qf, kept, top, total):
    tile = pl.program_id(1)
    start, count = spans[tile, 0], spans[tile, 1]
    both = jnp.concatenate([q_ref[...], f_ref[...]], axis=1)
    for h in range(PER_HALF):
        qf[h] = both * head_lanes(h)
        top[h] = jnp.full((TILE, HALF), -3e38, jnp.float32)
        total[h] = jnp.zeros((TILE, HALF), jnp.float32)

    def score_chunk(c, carry):
        kg = kg_ref[pl.ds(pl.multiple_of(start + c * CHUNK, 16), CHUNK), :]
        for h in range(PER_HALF):
            scores = against_rows(qf[h], kg)
            kept[c, h] = scores
            top[h] = jnp.maximum(top[h], jnp.maximum(scores[:, :HALF], scores[:, HALF:]))
        return carry

    lax.fori_loop(0, count, score_chunk, 0)
    for h in range(PER_HALF):
        top[h] = jnp.broadcast_to(jnp.max(top[h], axis=1, keepdims=True), (TILE, HALF))

    def weigh_chunk(c, acc):
        values = v_ref[pl.ds(pl.multiple_of(start + c * CHUNK, 16), CHUNK), :]
        for h in range(PER_HALF):
            shift = top[h]
            left = jnp.exp(kept[c, h, :, :HALF] - shift)
            right = jnp.exp(kept[c, h, :, HALF:] - shift)
            total[h] += left + right
            weights = jnp.concatenate([left, right], axis=1).astype(jnp.bfloat16)
            acc = acc + jnp.dot(
                weights, values * head_lanes(h)[:, :HALF], preferred_element_type=jnp.float32
            )
        return acc

    acc = lax.fori_loop(0, count, weigh_chunk, jnp.zeros((TILE, HALF), jnp.float32))
    lane = lax.broadcasted_iota(jnp.int32, (1, HALF), 1)
    factor = jnp.zeros((TILE, HALF), jnp.float32)
    logs = []
    for h in range(PER_HALF):
        row_total = jnp.sum(total[h], axis=1, keepdims=True)
        factor = jnp.where(lane // HEAD_SIZE == h, 1.0 / row_total, factor)
        logs.append(-(top[h][:, :1] + jnp.log(row_total)))
    att_ref[...] = (acc * factor).astype(jnp.bfloat16)
    logs_ref[...] = (f_ref[...].astype(jnp.float32) + three_terms(logs)).astype(jnp.bfloat16)


def attend(spans, queries, marks_f, keys_g, values):
    return pl.pallas_call(
        forward_kernel,
        grid=(2, 2),
        out_shape=[
            jax.ShapeDtypeStruct((512, 256), jnp.bfloat16),
            jax.ShapeDtypeStruct((2, 512, HALF), jnp.bfloat16),
        ],
        in_specs=[
            pl.BlockSpec(memory_space=pltpu.SMEM),
            pl.BlockSpec((TILE, HALF), lambda g, t: (t, g)),
            pl.BlockSpec((TILE, HALF), lambda g, t: (t, 0)),
            pl.BlockSpec((None, WINDOW, 2 * HALF), lambda g, t: (g, 0, 0)),
            pl.BlockSpec((WINDOW, HALF), lambda g, t: (0, g)),
        ],
        out_specs=[
            pl.BlockSpec((TILE, HALF), lambda g, t: (t, g)),
            pl.BlockSpec((None, TILE, HALF), lambda g, t: (g, t, 0)),
        ],
        scratch_shapes=[
            pltpu.VMEM((PER_HALF, TILE, 2 * HALF), jnp.bfloat16),
            pltpu.VMEM((WINDOW // CHUNK, PER_HALF, TILE, CHUNK), jnp.float32),
            pltpu.VMEM((PER_HALF, TILE, HALF), jnp.float32),
            pltpu.VMEM((PER_HALF, TILE, HALF), jnp.float32),
        ],
        compiler_params=pltpu.CompilerParams(vmem_limit_bytes=48 * 1024 * 1024),
        name="attention",
    )(spans, queries, marks_f, keys_g, values)


def backward_kernel(
    spans, q_ref, logs_ref, do_ref, deltas_ref, kg_ref, vg_ref, dq_ref, dk_ref, dv_ref, qf, df, dqt
):
    tile = pl.program_id(1)
    start, count = spans[tile, 0], spans[tile, 1]
    q_both = jnp.concatenate([q_ref[...], logs_ref[...]], axis=1)
    d_both = jnp.concatenate([do_ref[...], deltas_ref[...]], axis=1)
    for h in range(PER_HALF):
        lanes = head_lanes(h)
        qf[h] = q_both * lanes
        df[h] = d_both * lanes
    dqt[...] = jnp.zeros_like(dqt)

    @pl.when(tile == 0)
    def _():
        dk_ref[...] = jnp.zeros_like(dk_ref)
        dv_ref[...] = jnp.zeros_like(dv_ref)

    def chunk(c, carry):
        rows = pl.ds(pl.multiple_of(start + c * CHUNK, 16), CHUNK)
        kg = kg_ref[rows, :]
        vg = vg_ref[rows, :]
        keys_t = kg[:, :HALF].astype(jnp.float32).T.astype(jnp.bfloat16)
        dk = jnp.zeros((CHUNK, HALF), jnp.float32)
        dv = jnp.zeros((CHUNK, HALF), jnp.float32)
        for h in range(PER_HALF):
            weights = jnp.exp(against_rows(kg, qf[h]))
            dscores = (weights * against_rows(vg, df[h])).astype(jnp.bfloat16)
            dk = dk + jnp.dot(dscores, qf[h, :, :HALF], preferred_element_type=jnp.float32)
            dv = dv + jnp.dot(
                weights.astype(jnp.bfloat16), df[h, :, :HALF], preferred_element_type=jnp.float32
            )
            own = slice(h * HEAD_SIZE, (h + 1) * HEAD_SIZE)
            dqt[own, :] += jnp.dot(keys_t[own], dscores, preferred_element_type=jnp.float32)
        dk_ref[rows, :] += dk * 4.0
        dv_ref[rows, :] += dv * 4.0
        return carry

    lax.fori_loop(0, count, chunk, 0)
    dq_ref[...] = dqt[...].T.astype(jnp.bfloat16)


def attend_back(spans, queries, logs, douts, deltas, keys_g, values_g):
    tall = pl.BlockSpec((None, WINDOW, 2 * HALF), lambda g, t: (g, 0, 0))
    mine = pl.BlockSpec((TILE, HALF), lambda g, t: (t, g))
    terms = pl.BlockSpec((None, TILE, HALF), lambda g, t: (g, t, 0))
    sums = pl.BlockSpec((WINDOW, HALF), lambda g, t: (0, g))
    return pl.pallas_call(
        backward_kernel,
        grid=(2, 2),
        out_shape=[
            jax.ShapeDtypeStruct((512, 256), jnp.bfloat16),
            jax.ShapeDtypeStruct((WINDOW, 256), jnp.float32),
            jax.ShapeDtypeStruct((WINDOW, 256), jnp.float32),
        ],
        in_specs=[pl.BlockSpec(memory_space=pltpu.SMEM), mine, terms, mine, terms, tall, tall],
        out_specs=[mine, sums, sums],
        scratch_shapes=[
            pltpu.VMEM((PER_HALF, TILE, 2 * HALF), jnp.bfloat16),
            pltpu.VMEM((PER_HALF, TILE, 2 * HALF), jnp.bfloat16),
            pltpu.VMEM((HALF, TILE), jnp.float32),
        ],
        compiler_params=pltpu.CompilerParams(vmem_limit_bytes=48 * 1024 * 1024),
        name="attention_back",
    )(spans, queries, logs, douts, deltas, keys_g, values_g)


MESH = pl.DeviceIdType.MESH
RANKS = 8
UNIT = 128
SHARD = 3 * UNIT
PIECE = SHARD // RANKS
EXTRA = 16


def places():
    me = lax.axis_index("pts")
    core, z, y, x = me % 2, (me // 2) % 8, (me // 16) % 8, me // 128
    wide = (x * 2 + core, lambda r: (r // 2) * 128 + y * 16 + z * 2 + r % 2)
    middle = (y, lambda r: x * 128 + r * 16 + z * 2 + core)
    near = (z, lambda r: x * 128 + y * 16 + r * 2 + core)
    return wide, middle, near


def swap(place, source, landing, send_sem, recv_sem):
    rank, device = place
    copies = []
    for k in range(1, RANKS):
        peer = (rank + k) % RANKS
        copy = pltpu.make_async_remote_copy(
            src_ref=source(peer),
            dst_ref=landing(rank),
            send_sem=send_sem.at[k - 1],
            recv_sem=recv_sem.at[k - 1],
            device_id=(device(peer),),
            device_id_type=MESH,
        )
        copy.start()
        copies.append(copy)
    return copies


def greet(groups):
    barrier = pltpu.get_barrier_semaphore()
    for rank, device in groups:
        for k in range(1, RANKS):
            pl.semaphore_signal(
                barrier, inc=1, device_id=(device((rank + k) % RANKS),), device_id_type=MESH
            )
    pl.semaphore_wait(barrier, len(groups) * (RANKS - 1))


def slot_sum(ref, start, size):
    total = ref[0, start : start + size, :].astype(jnp.float32)
    for r in range(1, RANKS):
        total = total + ref[r, start : start + size, :].astype(jnp.float32)
    return total


def reduce_kernel(
    scale, gq, go, gn, gp, gb, gg, oq, oo, on, op, ob, og,
    send_a, recv_a, send_b, recv_b, recv_c, gather_b, gather_a, send_sems, recv_sems,
):
    wide, middle, near = places()
    for unit in range(24):
        column = unit // 2 * UNIT
        rows = slice(unit % 2 * UNIT, unit % 2 * UNIT + UNIT)
        if column < 768:
            block = gq[rows, column : column + UNIT]
        elif column < 1024:
            block = go[rows, column - 768 : column - 768 + UNIT]
        else:
            block = gp[rows, column - 1024 : column - 1024 + UNIT]
        start = unit % 3 * UNIT
        send_a[unit // 3, start : start + UNIT, :] = (block * scale).astype(jnp.bfloat16)
    pieces = [gn[:, i * UNIT : (i + 1) * UNIT] for i in range(2)]
    pieces += [gb[:, i * UNIT : (i + 1) * UNIT] for i in range(4)]
    pieces += [gg[:, i * UNIT : (i + 1) * UNIT] for i in range(4)]
    pieces += [jnp.zeros((EXTRA - 10, UNIT), jnp.float32)]
    extra = (jnp.concatenate(pieces, axis=0) * scale).astype(jnp.bfloat16)
    for r in range(RANKS):
        send_a[r, SHARD:, :] = extra
    greet((wide, middle, near))

    copies = swap(wide, lambda r: send_a.at[r], lambda r: recv_a.at[r], send_sems.at[0], recv_sems.at[0])
    recv_a[wide[0]] = send_a[wide[0]]
    for copy in copies:
        copy.wait()
    extra = slot_sum(recv_a, SHARD, EXTRA).astype(jnp.bfloat16)
    for r in range(RANKS):
        send_b[r, :PIECE, :] = slot_sum(recv_a, r * PIECE, PIECE).astype(jnp.bfloat16)
        send_b[r, PIECE:, :] = extra

    copies = swap(middle, lambda r: send_b.at[r], lambda r: recv_b.at[r], send_sems.at[1], recv_sems.at[1])
    recv_b[middle[0]] = send_b[middle[0]]
    for copy in copies:
        copy.wait()
    recv_c[near[0]] = slot_sum(recv_b, 0, PIECE + EXTRA).astype(jnp.bfloat16)

    copies = swap(near, lambda r: recv_c.at[near[0]], lambda r: recv_c.at[r], send_sems.at[2], recv_sems.at[2])
    for copy in copies:
        copy.wait()
    total = slot_sum(recv_c, 0, PIECE + EXTRA)
    gather_b[middle[0]] = total[:PIECE].astype(jnp.bfloat16)

    copies = swap(middle, lambda r: gather_b.at[middle[0]], lambda r: gather_b.at[r], send_sems.at[3], recv_sems.at[3])
    extra = total[PIECE:]
    for i in range(2):
        on[:, i * UNIT : (i + 1) * UNIT] = extra[i : i + 1]
    for i in range(4):
        ob[:, i * UNIT : (i + 1) * UNIT] = extra[2 + i : 3 + i]
        og[:, i * UNIT : (i + 1) * UNIT] = extra[6 + i : 7 + i]
    for copy in copies:
        copy.wait()
    gather_a[wide[0]] = gather_b[...]
    copies = swap(wide, lambda r: gather_b, lambda r: gather_a.at[r], send_sems.at[4], recv_sems.at[4])
    for copy in copies:
        copy.wait()
    for unit in range(24):
        column = unit // 2 * UNIT
        first = unit % 2 * UNIT
        for part in range(8):
            at = unit % 3 * UNIT + part * 16
            block = gather_a[unit // 3, at // PIECE, at % PIECE : at % PIECE + 16, :].astype(jnp.float32)
            rows = slice(first + part * 16, first + part * 16 + 16)
            if column < 768:
                oq[rows, column : column + UNIT] = block
            elif column < 1024:
                oo[rows, column - 768 : column - 768 + UNIT] = block
            else:
                op[rows, column - 1024 : column - 1024 + UNIT] = block


def reduce_all(scale, grad_qkv, grad_out, grad_gain, grad_pool, grad_bias, grad_pgain):
    arrays = (grad_qkv, grad_out, grad_gain, grad_pool, grad_bias, grad_pgain)
    vmem = pl.BlockSpec(memory_space=pltpu.VMEM)
    half = jnp.bfloat16
    return pl.pallas_call(
        functools.partial(reduce_kernel, scale),
        out_shape=[jax.ShapeDtypeStruct(a.shape, jnp.float32) for a in arrays],
        in_specs=[vmem] * 6,
        out_specs=[vmem] * 6,
        scratch_shapes=[
            pltpu.VMEM((RANKS, SHARD + EXTRA, UNIT), half),
            pltpu.VMEM((RANKS, SHARD + EXTRA, UNIT), half),
            pltpu.VMEM((RANKS, PIECE + EXTRA, UNIT), half),
            pltpu.VMEM((RANKS, PIECE + EXTRA, UNIT), half),
            pltpu.VMEM((RANKS, PIECE + EXTRA, UNIT), half),
            pltpu.VMEM((RANKS, PIECE, UNIT), half),
            pltpu.VMEM((RANKS, RANKS, PIECE, UNIT), half),
            pltpu.SemaphoreType.DMA((5, RANKS - 1)),
            pltpu.SemaphoreType.DMA((5, RANKS - 1)),
        ],
        compiler_params=pltpu.CompilerParams(
            collective_id=5, has_side_effects=True, vmem_limit_bytes=24 * 1024 * 1024
        ),
        name="parameter_gradients",
    )(*arrays)


def key_spans(patch_marks, marks_ext):
    spans = []
    for t in range(2):
        first, last = patch_marks[t * TILE], patch_marks[(t + 1) * TILE - 1]
        low = jnp.sum((marks_ext[: 2 * PATCH] < first).astype(jnp.int32))
        upper = marks_ext[PATCH:]
        high = PATCH + jnp.sum(((upper > 0) & (upper <= last)).astype(jnp.int32))
        low = low // 16 * 16
        count = (high - low + CHUNK - 1) // CHUNK
        spans.append(jnp.stack([jnp.minimum(low, WINDOW - count * CHUNK), count]))
    return jnp.stack(spans)


def mark_digits(marks):
    lane = jnp.arange(HALF, dtype=jnp.int32)[None, :]
    high, low = marks[:, None] // DIGIT, marks[:, None] % DIGIT
    return jnp.where(lane < DIGIT, lane == high, lane - DIGIT == low) & (lane < LOG_LANE)


def body(
    points, patch_ids, cell_ids, norm_gain, w_qkv, w_out, w_pool, b_pool, pool_gain, cotangent
):
    row_count, feat_width = points.shape
    cell_count = cotangent.shape[0]
    lane = jnp.arange(HALF, dtype=jnp.int32)[None, :]
    patch_marks = patch_ids + 1
    marks_ext = padded(patch_marks, (("pts", 0),), PATCH)
    points_ext = padded(points, (("pts", 0),), PATCH)
    spans = key_spans(patch_marks, marks_ext)
    digits = mark_digits(marks_ext)
    terms_on = (lane >= LOG_LANE) & (lane < LOG_LANE + 24)
    marks_g = (digits | terms_on).astype(jnp.bfloat16)
    own_digits = digits[PATCH : PATCH + row_count]
    marks_f = jnp.where(own_digits | (lane >= LOG_LANE), 0.0, -FAR).astype(jnp.bfloat16)
    normed_ext, inv_ext = layer_stats(points_ext.astype(jnp.float32))
    hidden_ext = (normed_ext * norm_gain).astype(jnp.bfloat16)
    qkv_ext = jnp.dot(hidden_ext, w_qkv, preferred_element_type=jnp.float32).astype(jnp.bfloat16)
    own = slice(PATCH, PATCH + row_count)
    feats = points.astype(jnp.float32)
    normed, inv_std, hidden = normed_ext[own], inv_ext[own], hidden_ext[own]
    queries = qkv_ext[own, :feat_width] * jnp.bfloat16(0.25)
    keys_g = jnp.stack(
        [jnp.concatenate([qkv_ext[:, 256 + g * HALF : 384 + g * HALF], marks_g], axis=1) for g in range(2)]
    )
    values = qkv_ext[:, 2 * feat_width :]
    values_g = jnp.stack(
        [jnp.concatenate([values[:, g * HALF : (g + 1) * HALF], marks_g], axis=1) for g in range(2)]
    )
    attended, logs = attend(spans, queries, marks_f, keys_g, values)

    mixed = (feats + jnp.dot(attended, w_out, preferred_element_type=jnp.float32)).astype(
        jnp.bfloat16
    )
    local_cells = cell_ids - lax.axis_index("pts") * cell_count
    slots = jnp.arange(cell_count, dtype=jnp.int32)
    member = slots[:, None] == local_cells[None, :]
    sums = jnp.dot(member.astype(jnp.bfloat16), mixed, preferred_element_type=jnp.float32)
    counts = jnp.sum(member.astype(jnp.float32), axis=1)
    leading = local_cells < 0
    lead_sum = jnp.dot(
        leading.astype(jnp.bfloat16)[None, :], mixed, preferred_element_type=jnp.float32
    )
    lead_count = jnp.sum(leading.astype(jnp.float32))
    lead_pack = jnp.concatenate(
        [lead_sum, jnp.full((1, feat_width), lead_count, jnp.float32)], axis=0
    )
    from_next = from_behind(lead_pack, "pts", -1)
    sums_all = sums.at[cell_count - 1].add(from_next[0])
    counts_all = counts.at[cell_count - 1].add(from_next[1, 0])
    pooled_mean, pooled_normed, slope_grad, grad_pre, grad_pre_b, share = pool_rows(
        sums_all, counts_all, w_pool, b_pool, pool_gain, cotangent
    )
    lead_share = from_behind(share[cell_count - 1 :], "pts", 1)[0]
    grad_w_pool = inner_rows(pooled_mean, grad_pre_b)
    grad_b_pool = jnp.sum(grad_pre, axis=0)
    grad_pool_gain = jnp.sum(slope_grad * pooled_normed, axis=0)
    dmixed = jnp.where(
        leading[:, None], lead_share[None, :], jnp.take(share, jnp.maximum(local_cells, 0), axis=0)
    )
    dmixed_b = dmixed.astype(jnp.bfloat16)
    grad_w_out = inner_rows(attended, dmixed_b)
    grad_scale = 1.0 / math.sqrt(row_count * lax.axis_size("pts"))
    dattended = against_rows(dmixed_b, w_out).astype(jnp.bfloat16)
    deltas = jnp.sum(
        (dattended.astype(jnp.float32) * attended.astype(jnp.float32)).reshape(row_count, 2, PER_HALF, HEAD_SIZE),
        axis=-1,
    ) * -0.25
    first = deltas.astype(jnp.bfloat16)
    second = (deltas - first.astype(jnp.float32)).astype(jnp.bfloat16)
    third = (deltas - first.astype(jnp.float32) - second.astype(jnp.float32)).astype(jnp.bfloat16)
    zeros = jnp.zeros((2, row_count, LOG_LANE), jnp.bfloat16)
    delta_terms = jnp.concatenate(
        [zeros] + [jnp.moveaxis(part, 1, 0) for part in (first, second, third)] + [zeros[:, :, :40]], axis=2
    )
    dquery, dkey_ext, dvalue_ext = attend_back(
        spans, queries, logs, dattended * jnp.bfloat16(0.25), delta_terms, keys_g, values_g
    )
    dkv_ext = jnp.concatenate([dkey_ext, dvalue_ext], axis=1)
    rim_pack = jnp.concatenate([dkv_ext[:PATCH], dkv_ext[PATCH + row_count :]], axis=0)
    rim_back = padded(rim_pack.astype(jnp.bfloat16), (("pts", 0),), PATCH).astype(jnp.float32)
    from_prev = rim_back[:PATCH]
    from_next_rows = rim_back[3 * PATCH :]
    dkv_own = dkv_ext[PATCH : PATCH + row_count] + from_prev + from_next_rows
    dqkv = jnp.concatenate([dquery, dkv_own.astype(jnp.bfloat16)], axis=1)
    grad_qkv = inner_rows(hidden, dqkv)
    dhidden = against_rows(dqkv, w_qkv)
    grad_norm_gain = jnp.sum(dhidden * normed, axis=0)
    grad_points = dmixed + norm_back(dhidden * norm_gain, normed, inv_std)
    summed = reduce_all(
        grad_scale, grad_qkv, grad_w_out, grad_norm_gain[None], grad_w_pool, grad_b_pool[None], grad_pool_gain[None]
    )
    return (grad_points, summed[0], summed[1], summed[2][0], summed[3], summed[4][0], summed[5][0])


def solution(mesh):
    in_specs = (P("pts", None), P("pts"), P("pts"), P(), P(), P(), P(), P(), P(), P("pts", None))
    out_specs = (P("pts", None), P(), P(), P(), P(), P(), P())
    return jax.shard_map(body, mesh=mesh, in_specs=in_specs, out_specs=out_specs, check_vma=False)
```

time: 637 us -> 208 us (0.33)
  waiting for transfers between devices: 175 us -> 7.49 us
  matrix products: 171 us -> 5.82 us
  Pallas kernels: 0 us -> 122 us
  blocking collectives: 120 us -> 0 us
  other arithmetic: 68.8 us -> 18.1 us
  local copies, waits for them, and re-layouts: 55.9 us -> 19.8 us
  between operations: 14.7 us -> 7.9 us
    psum x1 -> x0, waiting for transfers between devices: 170 us -> none  [body(): lax.psum((grad_qkv, grad_norm_gain, grad_w_pool, grad_b_pool, grad_pool_g...]
    dot_general x57 -> x1, matrix products: 158 us -> 0.83 us  [body(): jnp.dot(hidden_ext, w_qkv, preferred_element_type=jnp.float32)]
    pallas_call x0 -> x3, Pallas kernels: none -> 122 us  [the longest x1 66.7 us: reduce_all(): pl.pallas_call(functools.partial(reduce_kernel, scale), out_shape=[jax.Sh...]
    psum x1 -> x0, blocking collectives: 120 us -> none  [body(): lax.psum((grad_qkv, grad_norm_gain, grad_w_pool, grad_b_pool, grad_pool_g...]
    dynamic_slice x40 -> x0, local copies, waits for them, and re-layouts: 41.8 us -> none  [the longest x8 13.1 us: tiles(): lax.dynamic_slice(kv_ext, (start, feat_width + column), (key_window, lane...]
    reduce_sum x8 -> x2, other arithmetic: 31.4 us -> 4.42 us  [the longest x1 3.28 us: key_spans(): low = jnp.sum((marks_ext[:2 * PATCH] < first).astype(jnp.int32))]
    eq x16 -> x0, other arithmetic: 8.07 us -> none  [tiles(): visible = (patch_marks[:, None] == marks_ext[None, :])[None]]
    unnamed x62 -> x59, local copies, waits for them, and re-layouts: 0.16 us -> 7.86 us
  transfers between devices with their start and end apart: 9 -> 8, of which waited for: 4 -> 3; matrix products, arithmetic and copies ran while one was open for 3% -> 7% of each run, Pallas kernels for 0% -> 0%
where the time goes in v1:
time: 208 us; the launch traced here: 207 us
  Pallas kernels  122 us (59%)
  starting transfers between devices  25.5 us (12%)
  local copies, waits for them, and re-layouts  19.8 us (10%)
  other arithmetic  18.1 us (9%)
  between operations  7.9 us (4%)
  waiting for transfers between devices  7.49 us (4%)
  matrix products  5.82 us (3%)
    pallas_call x1, Pallas kernels, reduce_all(): pl.pallas_call(functools.partial(reduce_kernel, scale), out_shape=[jax.Sh...  66.7 us
    pallas_call x1, Pallas kernels, attend_back(): pl.pallas_call(backward_kernel, grid=(2, 2), out_shape=[jax.ShapeDtypeStr...  35.3 us
    pallas_call x1, Pallas kernels, attend(): pl.pallas_call(forward_kernel, grid=(2, 2), out_shape=[jax.ShapeDtypeStru...  20.5 us
    ppermute x3, starting transfers between devices, padded(): lax.ppermute(lax.slice_in_dim(block, block.shape[dim] - width, None, axis...  12.8 us
    ppermute x3, starting transfers between devices, padded(): lax.ppermute(lax.slice_in_dim(block, 0, width, axis=dim), axis, backward)  8.66 us
    unnamed x59, local copies, waits for them, and re-layouts  7.86 us
  transfers between devices with their start and end apart: 8, of which 3 were waited for; matrix products, arithmetic and copies ran while one was open for 7% of the time, Pallas kernels for 0%

profile of v1, /device:TPU:1, one launch (start us, length us, event | category | flops | bytes accessed | tf_op | source)
XLA Modules:
  0.0 207.1 jit_solution(8765118534811791119)
XLA Ops:
  0.6 0.7 broadcast_add_fusion
  1.4 5.5 %collective-permute-start = (s32[512]{0:T(512)S(1)}, s32[512]{0:T(512)S(1)}, u32[]{:S(2)}, u32[]{:S(2)}) collective-permute-start(s32[512]{0:T(512)S(1)} %broadcast_add_fusion), channel_id=1, source_target_pairs={{0,1},{1,2},{2,3},{3,4},{4,5},{5,6},{6,7},{7,8},{8,9},{9,10},{10,1... | collective-permute-start | bytes 6152 | tf_op jit(solution)/shard_map/ppermute | solution.py:24
  6.9 4.7 %collective-permute-start.1 = (s32[512]{0:T(512)S(1)}, s32[512]{0:T(512)S(1)}, u32[]{:S(2)}, u32[]{:S(2)}) collective-permute-start(s32[512]{0:T(512)S(1)} %broadcast_add_fusion), channel_id=1, source_target_pairs={{1,0},{2,1},{3,2},{4,3},{5,4},{6,5},{7,6},{8,7},{9,8},{10,9},{11,1... | collective-permute-start | bytes 6152 | tf_op jit(solution)/shard_map/ppermute | solution.py:27
  11.6 1.1 copy.52
  12.7 1.9 collective-permute-start.3
  14.6 3.6 %collective-permute-start.2 = (bf16[512,256]{0,1:T(8,128)(2,1)S(1)}, bf16[512,256]{0,1:T(8,128)(2,1)S(1)}, u32[]{:S(2)}, u32[]{:S(2)}) collective-permute-start(bf16[512,256]{0,1:T(8,128)(2,1)S(1)} %copy.52), channel_id=1, source_target_pairs={{0,1},{1,2},{2,3},{3,4},{4,5},{5,6},{6,7},{7,8},{8,9},{9,10},{10,1... | collective-permute-start | bytes 786440 | tf_op jit(solution)/shard_map/ppermute | solution.py:24
  18.3 0.6 fusion.39
  18.9 1.2 broadcast_compare_fusion.1
  20.1 0.6 convert_reduce_fusion.6
  21.0 3.3 %convert_reduce_fusion.5 = (s32[]{:T(128)}, s32[]{:T(128)}, s32[]{:T(128)}, s32[]{:T(128)}) fusion(s32[512]{0:T(512)S(1)} %broadcast_add_fusion, s32[512]{0:T(512)S(1)} %collective-permute-done, s32[]{:T(128)} %bitcast, s32[]{:T(128)} %bitcast.5, s32[]{:T(128)} %bitcast.6, s32[512]{0:T(512)S(1)} %collective-permute-done.1, s32[]{:T(128)} %bitcast.1), kind=kLoop, calls=%fused_computation.94 | loop fusion | flops 17404 | bytes 6176 | tf_op jit(solution)/shard_map/reduce_sum | solution.py:410
  30.9 0.9 or_convert_fusion
  32.0 0.2 fusion.2
  32.3 1.4 fusion
  33.7 0.8 convolution_convert_fusion
  34.6 0.3 fusion.37
  34.9 1.4 fusion.8
  36.5 20.5 %attention.1 = (bf16[512,256]{1,0:T(8,128)(2,1)S(1)}, bf16[2,512,128]{2,1,0:T(8,128)(2,1)S(1)}) custom-call(s32[2,2]{1,0:T(2,128)S(1)} %pad_add_fusion.3.spans, bf16[512,256]{1,0:T(8,128)(2,1)S(1)} %slice_multiply_fusion.q_ref, bf16[512,128]{1,0:T(8,128)(2,1)S(1)} %select_convert_fusion.f_ref, bf16[2,1536,256]{2,1,0:T(8,128)(2,1)S(1)} %pad_maximum_fusion.kg_ref, ...), custom_call_target="tpu_custom_call" | custom-call | tf_op jit(solution)/shard_map/attention/pallas_call | solution.py:157
  57.1 0.2 fusion.3
  57.4 0.6 concatenate.75
  58.1 1.9 collective-permute-start.4
  60.2 2.8 %collective-permute-done.4 = f32[2,256]{1,0:T(2,128)S(1)} collective-permute-done((f32[2,256]{1,0:T(2,128)S(1)}, f32[2,256]{1,0:T(2,128)S(1)}, u32[]{:S(2)}, u32[]{:S(2)}) %collective-permute-start.4) | collective-permute-done | bytes 2080 | tf_op jit(solution)/shard_map/ppermute | solution.py:35
  63.0 0.5 slice.145
  63.6 0.8 fusion.29
  64.4 0.3 fusion.40
  64.9 0.3 multiply_reduce_fusion.3
  65.5 0.6 copy-done.11
  66.1 0.2 convolution_divide_fusion
  66.4 2.1 %collective-permute-start.5 = (f32[1,256]{1,0:T(1,128)S(1)}, f32[1,256]{1,0:T(1,128)S(1)}, u32[]{:S(2)}, u32[]{:S(2)}) collective-permute-start(f32[1,256]{1,0:T(1,128)S(1)} %slice.146), channel_id=1, source_target_pairs={{0,1},{1,2},{2,3},{3,4},{4,5},{5,6},{6,7},{7,8},{8,9},{9,10},{10,1... | collective-permute-start | bytes 3080 | tf_op jit(solution)/shard_map/ppermute | solution.py:35
  68.5 1.3 pad_maximum_fusion.1.vg_ref
  69.8 2.2 %gather_fusion = f32[512,256]{1,0:T(8,128)} fusion(f32[128,256]{1,0:T(8,128)S(1)} %convolution_divide_fusion, s32[1024]{0:T(1024)S(1)} %pad_clamp_fusion), kind=kCustom, calls=%fused_computation | custom fusion | bytes 1050624 | tf_op jit(solution)/shard_map/jit(_take)/gather | solution.py:483
  72.1 1.2 copy.56
  73.3 0.6 copy-done.15
  73.9 1.3 broadcast_multiply_fusion
  75.2 0.9 convert_multiply_fusion
  76.1 2.0 copy.58
  78.1 1.1 bitcast_reduce_fusion
  79.3 0.6 broadcast_multiply_fusion.1
  79.9 0.9 copy.59
  80.8 0.7 bitcast_convert_fusion
  81.6 0.9 subtract_convert_fusion
  82.5 0.7 slice.126
  83.2 1.6 concatenate.76.deltas_ref
  84.9 35.3 %attention_back.1 = (bf16[512,256]{1,0:T(8,128)(2,1)S(1)}, f32[1536,256]{1,0:T(8,128)S(1)}, f32[1536,256]{1,0:T(8,128)S(1)}) custom-call(s32[2,2]{1,0:T(2,128)S(1)} %pad_add_fusion.3.spans, bf16[512,256]{1,0:T(8,128)(2,1)S(1)} %slice_multiply_fusion.q_ref, bf16[2,512,128]{2,1,0:T(8,128)(2,1)S(1)} %get-tuple-element.43.logs_ref, ...), custom_call_target="tpu_custom_call" | custom-call | tf_op jit(solution)/shard_map/attention_back/pallas_call | solution.py:233
  120.1 0.2 constant_dynamic-update-slice_fusion.1
  120.4 0.2 constant_dynamic-update-slice_fusion
  121.0 2.1 collective-permute-start.7
  123.1 3.6 %collective-permute-start.6 = (bf16[512,512]{1,0:T(8,128)(2,1)S(1)}, bf16[512,512]{1,0:T(8,128)(2,1)S(1)}, u32[]{:S(2)}, u32[]{:S(2)}) collective-permute-start(bf16[512,512]{1,0:T(8,128)(2,1)S(1)} %get-tuple-element.111), channel_id=1, source_target_pairs={{0,1},{1,2},{2,3},{3,4},{4,5},{5,6},{6,7},{7,8},{8,9},{9,10},{10,1... | collective-permute-start | bytes 1572872 | tf_op jit(solution)/shard_map/ppermute | solution.py:24
  126.7 0.7 slice.147
  127.4 0.3 fusion.24.gp
  127.8 0.3 fusion.32.go
  128.1 3.5 %collective-permute-done.7 = bf16[512,512]{1,0:T(8,128)(2,1)S(1)} collective-permute-done((bf16[512,512]{1,0:T(8,128)(2,1)S(1)}, bf16[512,512]{1,0:T(8,128)(2,1)S(1)}, u32[]{:S(2)}, u32[]{:S(2)}) %collective-permute-start.7) | collective-permute-done | bytes 524320 | tf_op jit(solution)/shard_map/ppermute | solution.py:27
  131.6 1.2 collective-permute-done.6
  132.8 0.2 fusion.5
  133.0 1.4 fusion.12.gq
  134.5 0.5 multiply_reduce_fusion
  135.1 0.2 multiply_add_fusion
  135.3 1.0 copy.60
  136.3 66.7 %parameter_gradients.1 = (f32[256,768]{1,0:T(8,128)S(1)}, f32[256,256]{1,0:T(8,128)S(1)}, f32[1,256]{1,0:T(1,128)S(1)}, f32[256,512]{1,0:T(8,128)S(1)}, f32[1,512]{1,0:T(1,128)S(1)}, /*index=5*/f32[1,512]{1,0:T(1,128)S(1)}) custom-call(f32[256,768]{1,0:T(8,128)S(1)} %fusion.12.gq, f32[256,256]{1,0:T(8,128)S(1)} %fusion.32.go, f32[1,256]{1,0:T(1,128)S(1)} %bitcast.66, ...), custom_call_target="tpu_custom_call" | custom-call | tf_op jit(solution)/shard_map/parameter_gradients/pallas_call | solution.py:383
  203.0 0.9 copy.72
  203.9 0.7 copy.73
  204.6 0.6 copy.74
  205.1 0.8 copy.75
  205.9 0.6 copy.76
  206.5 0.6 copy.77
  (87 shorter events, 1.9 us)
Async XLA Ops:
  0.6 33.1 %copy-start = (bf16[256,768]{1,0:T(8,128)(2,1)S(1)}, bf16[256,768]{1,0:T(8,128)(2,1)}, u32[]{:S(2)}) copy-start(bf16[256,768]{1,0:T(8,128)(2,1)} %param.18) | copy-start | bytes 1179652
  1.4 30.9 %copy-start.19 = (f32[256]{0:T(256)S(1)}, f32[256]{0:T(256)}, u32[]{:S(2)}) copy-start(f32[256]{0:T(256)} %param.17) | copy-start | bytes 3076
  1.4 19.5 %collective-permute-start = (s32[512]{0:T(512)S(1)}, s32[512]{0:T(512)S(1)}, u32[]{:S(2)}, u32[]{:S(2)}) collective-permute-start(s32[512]{0:T(512)S(1)} %broadcast_add_fusion), channel_id=1, source_target_pairs={{0,1},{1,2},{2,3},{3,4},{4,5},{5,6},{6,7},{7,8},{8,9},{9,10},{10,1... | collective-permute-start | bytes 6152 | tf_op jit(solution)/shard_map/ppermute | solution.py:24
  6.9 14.0 %collective-permute-start.1 = (s32[512]{0:T(512)S(1)}, s32[512]{0:T(512)S(1)}, u32[]{:S(2)}, u32[]{:S(2)}) collective-permute-start(s32[512]{0:T(512)S(1)} %broadcast_add_fusion), channel_id=1, source_target_pairs={{1,0},{2,1},{3,2},{4,3},{5,4},{6,5},{7,6},{8,7},{9,8},{10,9},{11,1... | collective-permute-start | bytes 6152 | tf_op jit(solution)/shard_map/ppermute | solution.py:27
  12.7 19.2 %collective-permute-start.3 = (bf16[512,256]{0,1:T(8,128)(2,1)S(1)}, bf16[512,256]{0,1:T(8,128)(2,1)S(1)}, u32[]{:S(2)}, u32[]{:S(2)}) collective-permute-start(bf16[512,256]{0,1:T(8,128)(2,1)S(1)} %copy.52), channel_id=1, source_target_pairs={{1,0},{2,1},{3,2},{4,3},{5,4},{6,5},{7,6},{8,7},{9,8},{10,9},{11,1... | collective-permute-start | bytes 786440 | tf_op jit(solution)/shard_map/ppermute | solution.py:27
  14.6 17.2 %collective-permute-start.2 = (bf16[512,256]{0,1:T(8,128)(2,1)S(1)}, bf16[512,256]{0,1:T(8,128)(2,1)S(1)}, u32[]{:S(2)}, u32[]{:S(2)}) collective-permute-start(bf16[512,256]{0,1:T(8,128)(2,1)S(1)} %copy.52), channel_id=1, source_target_pairs={{0,1},{1,2},{2,3},{3,4},{4,5},{5,6},{6,7},{7,8},{8,9},{9,10},{10,1... | collective-permute-start | bytes 786440 | tf_op jit(solution)/shard_map/ppermute | solution.py:24
  32.3 1.4 copy-start.14
  33.7 0.9 copy-start.3
  36.5 20.6 %copy-start.7 = (bf16[512,256]{1,0:T(8,128)(2,1)S(1)}, bf16[512,256]{1,0:T(8,128)(2,1)}, u32[]{:S(2)}) copy-start(bf16[512,256]{1,0:T(8,128)(2,1)} %param.14) | copy-start | bytes 786436
  36.5 20.6 %copy-start.10 = (bf16[256,256]{1,0:T(8,128)(2,1)S(1)}, bf16[256,256]{1,0:T(8,128)(2,1)}, u32[]{:S(2)}) copy-start(bf16[256,256]{1,0:T(8,128)(2,1)} %param.19) | copy-start | bytes 393220
  36.5 27.8 %copy-start.23 = (bf16[256,512]{1,0:T(8,128)(2,1)S(1)}, bf16[256,512]{1,0:T(8,128)(2,1)}, u32[]{:S(2)}) copy-start(bf16[256,512]{1,0:T(8,128)(2,1)} %param.20) | copy-start | bytes 786436
  36.5 27.8 %copy-start.24 = (f32[512]{0:T(512)S(1)}, f32[512]{0:T(512)}, u32[]{:S(2)}) copy-start(f32[512]{0:T(512)} %param.21) | copy-start | bytes 6148
  57.0 7.9 %copy-start.13 = (f32[128,512]{1,0:T(8,128)S(1)}, f32[128,512]{1,0:T(8,128)}, u32[]{:S(2)}) copy-start(f32[128,512]{1,0:T(8,128)} %param.23) | copy-start | bytes 786436
  57.0 7.9 %copy-start.17 = (f32[512]{0:T(512)S(1)}, f32[512]{0:T(512)}, u32[]{:S(2)}) copy-start(f32[512]{0:T(512)} %param.22) | copy-start | bytes 6148
  58.1 4.9 %collective-permute-start.4 = (f32[2,256]{1,0:T(2,128)S(1)}, f32[2,256]{1,0:T(2,128)S(1)}, u32[]{:S(2)}, u32[]{:S(2)}) collective-permute-start(f32[2,256]{1,0:T(2,128)S(1)} %concatenate.75), channel_id=1, source_target_pairs={{1,0},{2,1},{3,2},{4,3},{5,4},{6,5},{7,6},{8,7},{9,8},{10,9},{11,1... | collective-permute-start | bytes 6152 | tf_op jit(solution)/shard_map/ppermute | solution.py:35
  63.0 2.5 %copy-start.8 = (f32[128,256]{1,0:T(8,128)}, f32[128,256]{1,0:T(8,128)S(1)}, u32[]{:S(2)}) copy-start(f32[128,256]{1,0:T(8,128)S(1)} %scatter-add.6) | copy-start | bytes 393220
  64.4 2.0 copy-start.21
  64.4 4.1 %copy-start.4 = (bf16[1,1536,256]{2,1,0:T(8,128)(2,1)S(1)}, bf16[1,1536,256]{2,1,0:T(8,128)(2,1)}, u32[]{:S(2)}) copy-start(bf16[1,1536,256]{2,1,0:T(8,128)(2,1)} %get-tuple-element.117) | copy-start | bytes 2359300
  64.4 4.1 %copy-start.5 = (bf16[1,1536,256]{2,1,0:T(8,128)(2,1)S(1)}, bf16[1,1536,256]{2,1,0:T(8,128)(2,1)}, u32[]{:S(2)}) copy-start(bf16[1,1536,256]{2,1,0:T(8,128)(2,1)} %get-tuple-element.119) | copy-start | bytes 2359300
  65.5 0.7 copy-start.11
  66.4 6.9 %collective-permute-start.5 = (f32[1,256]{1,0:T(1,128)S(1)}, f32[1,256]{1,0:T(1,128)S(1)}, u32[]{:S(2)}, u32[]{:S(2)}) collective-permute-start(f32[1,256]{1,0:T(1,128)S(1)} %slice.146), channel_id=1, source_target_pairs={{0,1},{1,2},{2,3},{3,4},{4,5},{5,6},{6,7},{7,8},{8,9},{9,10},{10,1... | collective-permute-start | bytes 3080 | tf_op jit(solution)/shard_map/ppermute | solution.py:35
  73.3 4.8 %copy-start.1 = (f32[512,256]{0,1:T(8,128)}, f32[512,256]{0,1:T(8,128)S(1)}, u32[]{:S(2)}) copy-start(f32[512,256]{0,1:T(8,128)S(1)} %copy.56) | copy-start | bytes 1572868
  73.3 0.6 copy-start.15
  120.8 6.5 %copy-start.9 = (f32[128,256]{1,0:T(8,128)S(1)}, f32[128,256]{1,0:T(8,128)}, u32[]{:S(2)}) copy-start(f32[128,256]{1,0:T(8,128)} %copy-done.8) | copy-start | bytes 393220
  120.9 6.5 %copy-start.12 = (bf16[128,512]{1,0:T(8,128)(2,1)S(1)}, bf16[128,512]{1,0:T(8,128)(2,1)}, u32[]{:S(2)}) copy-start(bf16[128,512]{1,0:T(8,128)(2,1)} %copy-done.11) | copy-start | bytes 393220
  120.9 6.5 %copy-start.22 = (f32[128]{0:T(128)S(1)}, f32[128]{0:T(128)}, u32[]{:S(2)}) copy-start(f32[128]{0:T(128)} %copy-done.21) | copy-start | bytes 1540
  120.9 6.8 %copy-start.2 = (f32[512,256]{0,1:T(8,128)S(1)}, f32[512,256]{0,1:T(8,128)}, u32[]{:S(2)}) copy-start(f32[512,256]{0,1:T(8,128)} %copy-done.1) | copy-start | bytes 1572868
  120.9 6.8 %copy-start.16 = (f32[1,256]{1,0:T(1,128)S(1)}, f32[1,256]{1,0:T(1,128)}, u32[]{:S(2)}) copy-start(f32[1,256]{1,0:T(1,128)} %copy-done.15) | copy-start | bytes 3076
  120.9 6.8 %copy-start.18 = (pred[512]{0:T(512)(128)(4,1)S(1)}, pred[512]{0:T(512)(128)(4,1)}, u32[]{:S(2)}) copy-start(pred[512]{0:T(512)(128)(4,1)} %get-tuple-element.102) | copy-start | bytes 1540
  121.0 10.6 %collective-permute-start.7 = (bf16[512,512]{1,0:T(8,128)(2,1)S(1)}, bf16[512,512]{1,0:T(8,128)(2,1)S(1)}, u32[]{:S(2)}, u32[]{:S(2)}) collective-permute-start(bf16[512,512]{1,0:T(8,128)(2,1)S(1)} %get-tuple-element.112), channel_id=1, source_target_pairs={{1,0},{2,1},{3,2},{4,3},{5,4},{6,5},{7,6},{8,7},{9,8},{10,9},{11,1... | collective-permute-start | bytes 1572872 | tf_op jit(solution)/shard_map/ppermute | solution.py:27
  123.1 9.8 %collective-permute-start.6 = (bf16[512,512]{1,0:T(8,128)(2,1)S(1)}, bf16[512,512]{1,0:T(8,128)(2,1)S(1)}, u32[]{:S(2)}, u32[]{:S(2)}) collective-permute-start(bf16[512,512]{1,0:T(8,128)(2,1)S(1)} %get-tuple-element.111), channel_id=1, source_target_pairs={{0,1},{1,2},{2,3},{3,4},{4,5},{5,6},{6,7},{7,8},{8,9},{9,10},{10,1... | collective-permute-start | bytes 1572872 | tf_op jit(solution)/shard_map/ppermute | solution.py:24
  133.0 1.5 copy-start.6
  133.0 1.5 copy-start.20

commit v2 on v1

v2 whole, which is shorter than its diff:
```python
import functools
import math

import jax
import jax.numpy as jnp
from jax import lax
from jax.experimental import pallas as pl
from jax.experimental.pallas import tpu as pltpu
from jax.sharding import PartitionSpec as P

PATCH = 512
MESH = pl.DeviceIdType.MESH


EPS = 1e-05
ROOT_HALF = 0.7071067811865476
ROOT_TWO_PI = 2.5066282746310002


def layer_stats(values):
    centered = values - jnp.mean(values, axis=-1, keepdims=True)
    inv_std = lax.rsqrt(jnp.mean(centered * centered, axis=-1, keepdims=True) + EPS)
    return (centered * inv_std, inv_std)


def norm_back(grad_normed, normed, inv_std):
    first_mean = jnp.mean(grad_normed, axis=-1, keepdims=True)
    second_mean = jnp.mean(grad_normed * normed, axis=-1, keepdims=True)
    return inv_std * (grad_normed - first_mean - normed * second_mean)


def gelu_slope(scaled):
    normal_cdf = 0.5 * (1.0 + lax.erf(scaled * ROOT_HALF))
    return normal_cdf + scaled * jnp.exp(-0.5 * scaled * scaled) / ROOT_TWO_PI


def inner_rows(left, right):
    return lax.dot_general(
        left, right, (((0,), (0,)), ((), ())), preferred_element_type=jnp.float32
    )


def against_rows(left, right):
    return lax.dot_general(
        left, right, (((1,), (1,)), ((), ())), preferred_element_type=jnp.float32
    )


HALF = 128
PER_HALF = 8
HEAD_SIZE = 16
TILE = 256
CHUNK = 256
WINDOW = 3 * PATCH
FAR = float(2**30)
DIGIT = 32
LOG_LANE = 64


def head_lanes(h):
    lane = lax.broadcasted_iota(jnp.int32, (1, 2 * HALF), 1)
    own = (lane >= h * HEAD_SIZE) & (lane < (h + 1) * HEAD_SIZE)
    marks = (lane >= HALF) & (lane < HALF + LOG_LANE)
    terms = (lane >= HALF + LOG_LANE) & (lane < HALF + LOG_LANE + 24) & (lane % PER_HALF == h)
    return (own | marks | terms).astype(jnp.float32).astype(jnp.bfloat16)


def three_terms(columns):
    lane = lax.broadcasted_iota(jnp.int32, (1, HALF), 1)
    placed = jnp.zeros((columns[0].shape[0], HALF), jnp.float32)
    for h, column in enumerate(columns):
        here = (lane >= LOG_LANE) & (lane < LOG_LANE + 24) & (lane % PER_HALF == h)
        placed = jnp.where(here, column, placed)
    first = placed.astype(jnp.bfloat16).astype(jnp.float32)
    second = (placed - first).astype(jnp.bfloat16).astype(jnp.float32)
    third = placed - first - second
    which = (lane - LOG_LANE) // PER_HALF
    return jnp.where(which == 0, first, jnp.where(which == 1, second, third))


def neighbours():
    me = lax.axis_index("pts")
    count = lax.axis_size("pts")
    return me, (me + count - 1) % count, (me + 1) % count


def greet_neighbours(before, after):
    barrier = pltpu.get_barrier_semaphore()
    for device in (before, after):
        pl.semaphore_signal(barrier, inc=1, device_id=(device,), device_id_type=MESH)
    pl.semaphore_wait(barrier, 2)


def send(source, landing, sems, index, device):
    copy = pltpu.make_async_remote_copy(
        src_ref=source,
        dst_ref=landing,
        send_sem=sems.at[0, index],
        recv_sem=sems.at[1, index],
        device_id=(device,),
        device_id_type=MESH,
    )
    copy.start()
    return copy


def digit_columns(marks):
    row = lax.broadcasted_iota(jnp.int32, (HALF, HALF), 0)
    high, low = marks // DIGIT, marks % DIGIT
    hit = ((row < DIGIT) & (row == high)) | ((row >= DIGIT) & (row < LOG_LANE) & (row - DIGIT == low))
    return hit.astype(jnp.float32).T


def prepare_kernel(
    points, ids, gain, w_qkv, q_ref, kg_ref, vg_ref, f_ref, hidden_ref, spans_ref,
    marks, marks_low, marks_high, rows_low, rows_high, sems,
):
    me, before, after = neighbours()
    marks[...] = jnp.zeros_like(marks)
    marks[:4, :] = ids[...] + 1
    greet_neighbours(before, after)
    copies = [
        send(points, rows_high, sems, 0, before),
        send(points, rows_low, sems, 1, after),
        send(marks, marks_high, sems, 2, before),
        send(marks, marks_low, sems, 3, after),
    ]

    def project(block, first, columns):
        normed, _ = layer_stats(block[...].astype(jnp.float32))
        hidden = (normed * gain[...]).astype(jnp.bfloat16)
        hidden_ref[first : first + PATCH, :] = hidden
        return jnp.dot(hidden, w_qkv[:, columns], preferred_element_type=jnp.float32)

    def place(first, keys, values):
        for g in range(2):
            lanes = slice(g * HALF, (g + 1) * HALF)
            kg_ref[g, first : first + PATCH, :HALF] = keys[:, lanes].astype(jnp.bfloat16)
            vg_ref[g, first : first + PATCH, :HALF] = values[:, lanes].astype(jnp.bfloat16)

    def place_marks(block, first, own):
        lane = lax.broadcasted_iota(jnp.int32, (HALF, HALF), 1)
        terms = (lane >= LOG_LANE) & (lane < LOG_LANE + 24)
        for i in range(4):
            rows = slice(first + i * HALF, first + (i + 1) * HALF)
            digits = digit_columns(block[i : i + 1, :])
            both = jnp.where(terms, 1.0, digits).astype(jnp.bfloat16)
            for g in range(2):
                kg_ref[g, rows, HALF:] = both
                vg_ref[g, rows, HALF:] = both
            if own:
                away = jnp.where(lane < LOG_LANE, (1.0 - digits) * -FAR, 0.0)
                f_ref[i * HALF : (i + 1) * HALF, :] = away.astype(jnp.bfloat16)

    qkv = project(points, PATCH, slice(None))
    q_ref[...] = (qkv[:, :256].astype(jnp.bfloat16).astype(jnp.float32) * 0.25).astype(jnp.bfloat16)
    place(PATCH, qkv[:, 256:512], qkv[:, 512:])
    own = marks[...]
    place_marks(own, PATCH, True)
    for copy in copies[2:]:
        copy.wait()
    low = jnp.where(me == 0, 0, marks_low[...])
    high = jnp.where(me == lax.axis_size("pts") - 1, 0, marks_high[...])
    place_marks(low, 0, False)
    place_marks(high, 2 * PATCH, False)
    own_f, low_f, high_f = (block[:4].astype(jnp.float32) for block in (own, low, high))
    for t in range(2):
        first = jnp.min(own_f[2 * t : 2 * t + 2])
        last = jnp.max(own_f[2 * t : 2 * t + 2])
        lower = jnp.sum((low_f < first).astype(jnp.float32) + (own_f < first).astype(jnp.float32))
        upper = jnp.sum(
            ((high_f > 0) & (high_f <= last)).astype(jnp.float32) + (own_f <= last).astype(jnp.float32)
        )
        lower = lower.astype(jnp.int32) // 16 * 16
        count = (PATCH + upper.astype(jnp.int32) - lower + CHUNK - 1) // CHUNK
        spans_ref[t, 0] = jnp.minimum(lower, WINDOW - count * CHUNK)
        spans_ref[t, 1] = count
    for copy, block, first in ((copies[1], rows_low, 0), (copies[0], rows_high, 2 * PATCH)):
        copy.wait()
        kv = project(block, first, slice(256, 768))
        place(first, kv[:, :256], kv[:, 256:])


def prepare(points, ids, gain, w_qkv):
    half = jnp.bfloat16
    vmem = pl.BlockSpec(memory_space=pltpu.VMEM)
    return pl.pallas_call(
        prepare_kernel,
        out_shape=[
            jax.ShapeDtypeStruct((PATCH, 256), half),
            jax.ShapeDtypeStruct((2, WINDOW, 2 * HALF), half),
            jax.ShapeDtypeStruct((2, WINDOW, 2 * HALF), half),
            jax.ShapeDtypeStruct((PATCH, HALF), half),
            jax.ShapeDtypeStruct((WINDOW, 256), half),
            jax.ShapeDtypeStruct((2, 2), jnp.int32),
        ],
        in_specs=[vmem] * 4,
        out_specs=[vmem] * 5 + [pl.BlockSpec(memory_space=pltpu.SMEM)],
        scratch_shapes=[
            pltpu.VMEM((8, HALF), jnp.int32),
            pltpu.VMEM((8, HALF), jnp.int32),
            pltpu.VMEM((8, HALF), jnp.int32),
            pltpu.VMEM((PATCH, 256), half),
            pltpu.VMEM((PATCH, 256), half),
            pltpu.SemaphoreType.DMA((2, 4)),
        ],
        compiler_params=pltpu.CompilerParams(
            collective_id=1, has_side_effects=True, vmem_limit_bytes=32 * 1024 * 1024
        ),
        name="prepare",
    )(points, ids, gain, w_qkv)


SLOTS = 144


def membership(cells):
    local = cells - lax.axis_index("pts") * HALF
    local = jnp.where(local < 0, HALF, local)
    slot = lax.broadcasted_iota(jnp.int32, (SLOTS, HALF), 0)
    parts = [(slot == local[i : i + 1, :]).astype(jnp.float32) for i in range(4)]
    return jnp.concatenate(parts, axis=1)


def forward_kernel(
    spans, q_ref, f_ref, kg_ref, vg_ref, points_ref, w_out_ref, cells_ref,
    att_ref, logs_ref, sums_ref, counts_ref, qf, kept, top, total,
):
    tile, half = pl.program_id(0), pl.program_id(1)
    start, count = spans[tile, 0], spans[tile, 1]
    both = jnp.concatenate([q_ref[...], f_ref[...]], axis=1)
    for h in range(PER_HALF):
        qf[h] = both * head_lanes(h)
        top[h] = jnp.full((TILE, HALF), -3e38, jnp.float32)
        total[h] = jnp.zeros((TILE, HALF), jnp.float32)

    def score_chunk(c, carry):
        kg = kg_ref[half, pl.ds(pl.multiple_of(start + c * CHUNK, 16), CHUNK), :]
        for h in range(PER_HALF):
            scores = against_rows(qf[h], kg)
            kept[c, h] = scores
            top[h] = jnp.maximum(top[h], jnp.maximum(scores[:, :HALF], scores[:, HALF:]))
        return carry

    lax.fori_loop(0, count, score_chunk, 0)
    for h in range(PER_HALF):
        top[h] = jnp.broadcast_to(jnp.max(top[h], axis=1, keepdims=True), (TILE, HALF))

    def weigh_chunk(c, acc):
        values = vg_ref[half, pl.ds(pl.multiple_of(start + c * CHUNK, 16), CHUNK), :HALF]
        for h in range(PER_HALF):
            shift = top[h]
            left = jnp.exp(kept[c, h, :, :HALF] - shift)
            right = jnp.exp(kept[c, h, :, HALF:] - shift)
            total[h] += left + right
            weights = jnp.concatenate([left, right], axis=1).astype(jnp.bfloat16)
            acc = acc + jnp.dot(
                weights, values * head_lanes(h)[:, :HALF], preferred_element_type=jnp.float32
            )
        return acc

    acc = lax.fori_loop(0, count, weigh_chunk, jnp.zeros((TILE, HALF), jnp.float32))
    lane = lax.broadcasted_iota(jnp.int32, (1, HALF), 1)
    factor = jnp.zeros((TILE, HALF), jnp.float32)
    logs = []
    for h in range(PER_HALF):
        row_total = jnp.sum(total[h], axis=1, keepdims=True)
        factor = jnp.where(lane // HEAD_SIZE == h, 1.0 / row_total, factor)
        logs.append(-(top[h][:, :1] + jnp.log(row_total)))
    attended = (acc * factor).astype(jnp.bfloat16)
    rows = pl.ds(pl.multiple_of(tile * TILE, TILE), TILE)
    for g in range(2):

        @pl.when(half == g)
        def _():
            att_ref[rows, g * HALF : (g + 1) * HALF] = attended

    logs_ref[...] = (f_ref[...].astype(jnp.float32) + three_terms(logs)).astype(jnp.bfloat16)

    @pl.when((tile == 1) & (half == 1))
    def _():
        mixed = points_ref[...].astype(jnp.float32) + jnp.dot(
            att_ref[...], w_out_ref[...], preferred_element_type=jnp.float32
        )
        member = membership(cells_ref[...])
        sums_ref[...] = jnp.dot(
            member.astype(jnp.bfloat16), mixed.astype(jnp.bfloat16), preferred_element_type=jnp.float32
        )
        counts_ref[...] = jnp.broadcast_to(jnp.sum(member, axis=1, keepdims=True), (SLOTS, HALF))


def attend(spans, queries, marks_f, keys_g, values_g, points, w_out, cells):
    def whole(*shape):
        return pl.BlockSpec(shape, lambda t, g: (0,) * len(shape))

    return pl.pallas_call(
        forward_kernel,
        grid=(2, 2),
        out_shape=[
            jax.ShapeDtypeStruct((PATCH, 256), jnp.bfloat16),
            jax.ShapeDtypeStruct((PATCH, 256), jnp.bfloat16),
            jax.ShapeDtypeStruct((SLOTS, 256), jnp.float32),
            jax.ShapeDtypeStruct((SLOTS, HALF), jnp.float32),
        ],
        in_specs=[
            pl.BlockSpec(memory_space=pltpu.SMEM),
            pl.BlockSpec((TILE, HALF), lambda t, g: (t, g)),
            pl.BlockSpec((TILE, HALF), lambda t, g: (t, 0)),
            whole(2, WINDOW, 2 * HALF),
            whole(2, WINDOW, 2 * HALF),
            whole(PATCH, 256),
            whole(256, 256),
            whole(4, HALF),
        ],
        out_specs=[
            whole(PATCH, 256),
            pl.BlockSpec((TILE, HALF), lambda t, g: (t, g)),
            whole(SLOTS, 256),
            whole(SLOTS, HALF),
        ],
        scratch_shapes=[
            pltpu.VMEM((PER_HALF, TILE, 2 * HALF), jnp.bfloat16),
            pltpu.VMEM((WINDOW // CHUNK, PER_HALF, TILE, CHUNK), jnp.float32),
            pltpu.VMEM((PER_HALF, TILE, HALF), jnp.float32),
            pltpu.VMEM((PER_HALF, TILE, HALF), jnp.float32),
        ],
        compiler_params=pltpu.CompilerParams(vmem_limit_bytes=48 * 1024 * 1024),
        name="attention",
    )(spans, queries, marks_f, keys_g, values_g, points, w_out, cells)


def split_three(values, which):
    first = values.astype(jnp.bfloat16).astype(jnp.float32)
    second = (values - first).astype(jnp.bfloat16).astype(jnp.float32)
    third = values - first - second
    return jnp.where(which == 0, first, jnp.where(which == 1, second, third))


def pool_kernel(
    scale, sums, counts, cells, att, w_out, w_pool, b_pool, pool_gain, cotangent,
    dmixed_ref, datt_ref, delta_ref, gw_pool, gw_out, gb_pool, g_gain,
    back_pack, ahead_pack, from_after, from_before, sems,
):
    me, before, after = neighbours()
    back_pack[:, :256] = sums[HALF : HALF + 8, :]
    back_pack[:, 256:] = counts[HALF : HALF + 8, :]
    ahead_pack[:, :256] = sums[HALF - 8 : HALF, :]
    ahead_pack[:, 256:384] = counts[HALF - 8 : HALF, :]
    ahead_pack[:, 384:] = cotangent[HALF - 8 :, :]
    greet_neighbours(before, after)
    copies = [
        send(back_pack, from_after, sems, 0, before),
        send(ahead_pack, from_before, sems, 1, after),
    ]
    member = membership(cells[...]).astype(jnp.bfloat16)
    for copy in copies:
        copy.wait()
    row = lax.broadcasted_iota(jnp.int32, (8, 1), 0)
    late, early = from_after[0:1, :], from_before[7:8, :]
    last_sum = sums[HALF - 8 : HALF, :] + jnp.where(row == 7, late[:, :256], 0.0)
    lead_sum = jnp.where(row == 0, sums[HALF : HALF + 8, :] + early[:, :256], 0.0)
    last_count = counts[HALF - 8 : HALF, :] + jnp.where(row == 7, late[:, 256:], 0.0)
    lead_count = jnp.where(row == 0, counts[HALF : HALF + 8, :] + early[:, 256:384], 0.0)
    spare = jnp.zeros((8, 256), jnp.float32)
    all_sums = jnp.concatenate([sums[: HALF - 8, :], last_sum, lead_sum, spare], axis=0)
    all_counts = jnp.concatenate(
        [counts[: HALF - 8, :], last_count, lead_count, spare[:, :HALF]], axis=0
    )[:, :1]
    all_counts = jnp.maximum(all_counts, 1.0)
    lead_cot = jnp.where(row == 0, early[:, 384:], 0.0)
    all_cot = jnp.concatenate([cotangent[...], lead_cot, jnp.zeros((8, 512), jnp.float32)], axis=0)

    pooled_mean = (all_sums / all_counts).astype(jnp.bfloat16)
    pre_norm = jnp.dot(pooled_mean, w_pool[...], preferred_element_type=jnp.float32) + b_pool[...]
    pooled_normed, pooled_inv = layer_stats(pre_norm)
    slope_grad = all_cot * gelu_slope(pooled_normed * pool_gain[...])
    grad_pre = norm_back(slope_grad * pool_gain[...], pooled_normed, pooled_inv)
    grad_pre_b = grad_pre.astype(jnp.bfloat16)
    share = against_rows(grad_pre_b, w_pool[...]) / all_counts
    share_b = share.astype(jnp.bfloat16)
    rest_b = (share - share_b.astype(jnp.float32)).astype(jnp.bfloat16)
    dmixed_main = inner_rows(member, share_b)
    dmixed_ref[...] = dmixed_main + inner_rows(member, rest_b)
    dmixed_b = dmixed_main.astype(jnp.bfloat16)
    datt = against_rows(dmixed_b, w_out[...]).astype(jnp.bfloat16)
    datt_f = datt.astype(jnp.float32)
    datt_ref[...] = (datt_f * 0.25).astype(jnp.bfloat16)
    product = datt_f * att[...].astype(jnp.float32)
    channel = lax.broadcasted_iota(jnp.int32, (256, 256), 0)
    lane = lax.broadcasted_iota(jnp.int32, (256, 256), 1)
    spot = lane % HALF - LOG_LANE
    place = (channel // HALF == lane // HALF) & (spot >= 0) & (spot < 24)
    place = (place & (spot % PER_HALF == channel % HALF // HEAD_SIZE)).astype(jnp.float32)
    place = place.astype(jnp.bfloat16)
    first = product.astype(jnp.bfloat16)
    second = product - first.astype(jnp.float32)
    second_b = second.astype(jnp.bfloat16)
    third_b = (second - second_b.astype(jnp.float32)).astype(jnp.bfloat16)
    deltas = jnp.dot(first, place, preferred_element_type=jnp.float32)
    deltas = deltas + jnp.dot(second_b, place, preferred_element_type=jnp.float32)
    deltas = deltas + jnp.dot(third_b, place, preferred_element_type=jnp.float32)
    which = (lax.broadcasted_iota(jnp.int32, (1, 256), 1) % HALF - LOG_LANE) // PER_HALF
    delta_ref[...] = split_three(deltas * -0.25, which).astype(jnp.bfloat16)
    gw_pool[...] = (inner_rows(pooled_mean[:HALF], grad_pre_b[:HALF]) * scale).astype(jnp.bfloat16)
    gw_out[...] = (inner_rows(att[...], dmixed_b) * scale).astype(jnp.bfloat16)
    gb_pool[...] = jnp.sum(grad_pre[:HALF], axis=0, keepdims=True) * scale
    g_gain[...] = jnp.sum(slope_grad[:HALF] * pooled_normed[:HALF], axis=0, keepdims=True) * scale


def pool(scale, *arrays):
    half = jnp.bfloat16
    vmem = pl.BlockSpec(memory_space=pltpu.VMEM)
    return pl.pallas_call(
        functools.partial(pool_kernel, scale),
        out_shape=[
            jax.ShapeDtypeStruct((PATCH, 256), jnp.float32),
            jax.ShapeDtypeStruct((PATCH, 256), half),
            jax.ShapeDtypeStruct((PATCH, 256), half),
            jax.ShapeDtypeStruct((256, 512), half),
            jax.ShapeDtypeStruct((256, 256), half),
            jax.ShapeDtypeStruct((1, 512), jnp.float32),
            jax.ShapeDtypeStruct((1, 512), jnp.float32),
        ],
        in_specs=[vmem] * 9,
        out_specs=[vmem] * 7,
        scratch_shapes=[
            pltpu.VMEM((8, 384), jnp.float32),
            pltpu.VMEM((8, 896), jnp.float32),
            pltpu.VMEM((8, 384), jnp.float32),
            pltpu.VMEM((8, 896), jnp.float32),
            pltpu.SemaphoreType.DMA((2, 2)),
        ],
        compiler_params=pltpu.CompilerParams(
            collective_id=2, has_side_effects=True, vmem_limit_bytes=32 * 1024 * 1024
        ),
        name="pooling",
    )(*arrays)


def backward_kernel(
    spans, q_ref, logs_ref, do_ref, deltas_ref, kg_ref, vg_ref, dq_ref, dk_ref, dv_ref, qf, df, dqt, dk_sum, dv_sum
):
    tile = pl.program_id(1)
    start, count = spans[tile, 0], spans[tile, 1]
    q_both = jnp.concatenate([q_ref[...], logs_ref[...]], axis=1)
    d_both = jnp.concatenate([do_ref[...], deltas_ref[...]], axis=1)
    for h in range(PER_HALF):
        lanes = head_lanes(h)
        qf[h] = q_both * lanes
        df[h] = d_both * lanes
    dqt[...] = jnp.zeros_like(dqt)

    @pl.when(tile == 0)
    def _():
        dk_sum[...] = jnp.zeros_like(dk_sum)
        dv_sum[...] = jnp.zeros_like(dv_sum)

    def chunk(c, carry):
        rows = pl.ds(pl.multiple_of(start + c * CHUNK, 16), CHUNK)
        kg = kg_ref[rows, :]
        vg = vg_ref[rows, :]
        keys_t = kg[:, :HALF].astype(jnp.float32).T.astype(jnp.bfloat16)
        dk = jnp.zeros((CHUNK, HALF), jnp.float32)
        dv = jnp.zeros((CHUNK, HALF), jnp.float32)
        for h in range(PER_HALF):
            weights = jnp.exp(against_rows(kg, qf[h]))
            dscores = (weights * against_rows(vg, df[h])).astype(jnp.bfloat16)
            dk = dk + jnp.dot(dscores, qf[h, :, :HALF], preferred_element_type=jnp.float32)
            dv = dv + jnp.dot(
                weights.astype(jnp.bfloat16), df[h, :, :HALF], preferred_element_type=jnp.float32
            )
            own = slice(h * HEAD_SIZE, (h + 1) * HEAD_SIZE)
            dqt[own, :] += jnp.dot(keys_t[own], dscores, preferred_element_type=jnp.float32)
        dk_sum[rows, :] += dk * 4.0
        dv_sum[rows, :] += dv * 4.0
        return carry

    lax.fori_loop(0, count, chunk, 0)
    dq_ref[...] = dqt[...].T.astype(jnp.bfloat16)

    @pl.when(tile == 1)
    def _():
        dk_ref[...] = dk_sum[...].astype(jnp.bfloat16)
        dv_ref[...] = dv_sum[...].astype(jnp.bfloat16)


def attend_back(spans, queries, logs, douts, deltas, keys_g, values_g):
    tall = pl.BlockSpec((None, WINDOW, 2 * HALF), lambda g, t: (g, 0, 0))
    mine = pl.BlockSpec((TILE, HALF), lambda g, t: (t, g))
    sums = pl.BlockSpec((WINDOW, HALF), lambda g, t: (0, g))
    return pl.pallas_call(
        backward_kernel,
        grid=(2, 2),
        out_shape=[
            jax.ShapeDtypeStruct((512, 256), jnp.bfloat16),
            jax.ShapeDtypeStruct((WINDOW, 256), jnp.bfloat16),
            jax.ShapeDtypeStruct((WINDOW, 256), jnp.bfloat16),
        ],
        in_specs=[pl.BlockSpec(memory_space=pltpu.SMEM), mine, mine, mine, mine, tall, tall],
        out_specs=[mine, sums, sums],
        scratch_shapes=[
            pltpu.VMEM((PER_HALF, TILE, 2 * HALF), jnp.bfloat16),
            pltpu.VMEM((PER_HALF, TILE, 2 * HALF), jnp.bfloat16),
            pltpu.VMEM((HALF, TILE), jnp.float32),
            pltpu.VMEM((WINDOW, HALF), jnp.float32),
            pltpu.VMEM((WINDOW, HALF), jnp.float32),
        ],
        compiler_params=pltpu.CompilerParams(vmem_limit_bytes=48 * 1024 * 1024),
        name="attention_back",
    )(spans, queries, logs, douts, deltas, keys_g, values_g)


UNIT = 128
EXTRA = 16
CORE_ROWS = 12 * UNIT
X_ROWS = CORE_ROWS // 4
Y_ROWS = X_ROWS // 8


def axes():
    me = lax.axis_index("pts")
    core, z, y, x = me % 2, (me // 2) % 8, (me // 16) % 8, me // 128
    return (
        (core, 2, lambda r: x * 128 + y * 16 + z * 2 + r),
        (x, 4, lambda r: r * 128 + y * 16 + z * 2 + core),
        (y, 8, lambda r: x * 128 + r * 16 + z * 2 + core),
        (z, 8, lambda r: x * 128 + y * 16 + r * 2 + core),
    )


def swap(axis, source, landing, sems, first):
    rank, size, device = axis
    copies = []
    for k in range(1, size):
        peer = (rank + k) % size
        copies.append(send(source(peer), landing(rank), sems, first + k - 1, device(peer)))
    return copies


def wait_all(copies):
    for copy in copies:
        copy.wait()


def slot_sum(ref, start, size):
    total = ref[0, start : start + size, :].astype(jnp.float32)
    for r in range(1, ref.shape[0]):
        total = total + ref[r, start : start + size, :].astype(jnp.float32)
    return total


def finish_kernel(
    scale, hidden, dq, dk, dv, dmixed, points, gain, w_qkv, gw_out, gw_pool, gb_pool, g_gain,
    grad_points, reduced, extras,
    low_k, low_v, high_k, high_v, send_c, recv_c, send_x, recv_x, send_y, recv_y, recv_z,
    gather_y, gather_x, gather_c, sems,
):
    me, before, after = neighbours()
    on_core, on_x, on_y, on_z = axes()
    barrier = pltpu.get_barrier_semaphore()
    greeted = [before, after]
    for rank, size, device in (on_core, on_x, on_y, on_z):
        greeted += [device((rank + k) % size) for k in range(1, size)]
    for device in greeted:
        pl.semaphore_signal(barrier, inc=1, device_id=(device,), device_id_type=MESH)

    def fill(block, first_unit):
        for column in range(block.shape[1] // UNIT):
            unit = first_unit + 2 * column
            start = unit % 12 * UNIT
            send_c[unit // 12, start : start + 2 * UNIT, :] = block[:, column * UNIT : (column + 1) * UNIT]

    fill(gw_out[...], 12)
    fill(gw_pool[...], 16)
    pieces = [gb_pool[:, i * UNIT : (i + 1) * UNIT] for i in range(4)]
    pieces += [g_gain[:, i * UNIT : (i + 1) * UNIT] for i in range(4)]
    pieces += [jnp.zeros((EXTRA - 8, UNIT), jnp.float32)]
    packed = jnp.concatenate(pieces, axis=0).astype(jnp.bfloat16)
    for r in range(2):
        send_c[r, CORE_ROWS:, :] = packed
    pl.semaphore_wait(barrier, len(greeted))
    rims = [
        send(dk.at[pl.ds(0, PATCH)], high_k, sems, 40, before),
        send(dv.at[pl.ds(0, PATCH)], high_v, sems, 41, before),
        send(dk.at[pl.ds(2 * PATCH, PATCH)], low_k, sems, 42, after),
        send(dv.at[pl.ds(2 * PATCH, PATCH)], low_v, sems, 43, after),
    ]
    own = slice(PATCH, 2 * PATCH)
    fill((inner_rows(hidden[own, :], dq[...]) * scale).astype(jnp.bfloat16), 0)
    fill((inner_rows(hidden[...], dk[...]) * scale).astype(jnp.bfloat16), 4)
    fill((inner_rows(hidden[...], dv[...]) * scale).astype(jnp.bfloat16), 8)

    copies = swap(on_core, lambda r: send_c.at[r], lambda r: recv_c, sems, 0)
    dhidden = against_rows(dq[...], w_qkv[:, :256])
    wait_all(copies)
    kept = send_c.at[on_core[0]]
    extra = (
        kept[CORE_ROWS:, :].astype(jnp.float32) + recv_c[CORE_ROWS:, :].astype(jnp.float32)
    ).astype(jnp.bfloat16)
    for r in range(4):
        rows = slice(r * X_ROWS, (r + 1) * X_ROWS)
        total = kept[rows, :].astype(jnp.float32) + recv_c[rows, :].astype(jnp.float32)
        send_x[r, :X_ROWS, :] = total.astype(jnp.bfloat16)
        send_x[r, X_ROWS:, :] = extra

    copies = swap(on_x, lambda r: send_x.at[r], lambda r: recv_x.at[r], sems, 1)
    recv_x[on_x[0]] = send_x[on_x[0]]
    wait_all(rims)
    for columns, mine, low, high in (
        (slice(256, 512), dk, low_k, high_k), (slice(512, 768), dv, low_v, high_v)
    ):
        total = mine[own, :].astype(jnp.float32) + low[...].astype(jnp.float32)
        total = (total + high[...].astype(jnp.float32)).astype(jnp.bfloat16)
        dhidden = dhidden + against_rows(total, w_qkv[:, columns])
    normed, inv_std = layer_stats(points[...].astype(jnp.float32))
    grad_points[...] = dmixed[...] + norm_back(dhidden * gain[...], normed, inv_std)
    wait_all(copies)
    extra = slot_sum(recv_x, X_ROWS, EXTRA).astype(jnp.bfloat16)
    for r in range(8):
        send_y[r, :Y_ROWS, :] = slot_sum(recv_x, r * Y_ROWS, Y_ROWS).astype(jnp.bfloat16)
        send_y[r, Y_ROWS:, :] = extra

    copies = swap(on_y, lambda r: send_y.at[r], lambda r: recv_y.at[r], sems, 4)
    recv_y[on_y[0]] = send_y[on_y[0]]
    wait_all(copies)
    recv_z[on_z[0]] = slot_sum(recv_y, 0, Y_ROWS + EXTRA).astype(jnp.bfloat16)

    wait_all(swap(on_z, lambda r: recv_z.at[on_z[0]], lambda r: recv_z.at[r], sems, 11))
    total = slot_sum(recv_z, 0, Y_ROWS + EXTRA)
    extras[...] = total[Y_ROWS:]
    gather_y[on_y[0]] = total[:Y_ROWS].astype(jnp.bfloat16)
    wait_all(swap(on_y, lambda r: gather_y.at[on_y[0]], lambda r: gather_y.at[r], sems, 18))
    gather_x[on_x[0]] = gather_y[...]
    copies = swap(on_x, lambda r: gather_y, lambda r: gather_x.at[r], sems, 25)
    wait_all(copies)
    gather_c[on_core[0]] = gather_x[...]
    wait_all(swap(on_core, lambda r: gather_x, lambda r: gather_c.at[r], sems, 28))
    for c in range(2):
        for r in range(4):
            for s in range(8):
                start = c * CORE_ROWS + r * X_ROWS + s * Y_ROWS
                reduced[start : start + Y_ROWS, :] = gather_c[c, r, s]


def finish(scale, *arrays):
    half = jnp.bfloat16
    vmem = pl.BlockSpec(memory_space=pltpu.VMEM)
    return pl.pallas_call(
        functools.partial(finish_kernel, scale),
        out_shape=[
            jax.ShapeDtypeStruct((PATCH, 256), jnp.float32),
            jax.ShapeDtypeStruct((2 * CORE_ROWS, UNIT), half),
            jax.ShapeDtypeStruct((EXTRA, UNIT), jnp.float32),
        ],
        in_specs=[vmem] * 12,
        out_specs=[vmem] * 3,
        scratch_shapes=[pltpu.VMEM((PATCH, 256), half)] * 4
        + [
            pltpu.VMEM((2, CORE_ROWS + EXTRA, UNIT), half),
            pltpu.VMEM((CORE_ROWS + EXTRA, UNIT), half),
            pltpu.VMEM((4, X_ROWS + EXTRA, UNIT), half),
            pltpu.VMEM((4, X_ROWS + EXTRA, UNIT), half),
            pltpu.VMEM((8, Y_ROWS + EXTRA, UNIT), half),
            pltpu.VMEM((8, Y_ROWS + EXTRA, UNIT), half),
            pltpu.VMEM((8, Y_ROWS + EXTRA, UNIT), half),
            pltpu.VMEM((8, Y_ROWS, UNIT), half),
            pltpu.VMEM((4, 8, Y_ROWS, UNIT), half),
            pltpu.VMEM((2, 4, 8, Y_ROWS, UNIT), half),
            pltpu.SemaphoreType.DMA((2, 44)),
        ],
        compiler_params=pltpu.CompilerParams(
            collective_id=3, has_side_effects=True, vmem_limit_bytes=40 * 1024 * 1024
        ),
        name="finish",
    )(*arrays)


def unpack_kernel(reduced, extras, gain, w_qkv, gq, go, gn, gp, gb, gg):
    weighted = jnp.zeros((256, UNIT), jnp.float32)
    for column in range(12):
        block = reduced[column * 256 : (column + 1) * 256, :].astype(jnp.float32)
        lanes = slice(column % 12 * UNIT, (column % 12 + 1) * UNIT)
        if column < 6:
            gq[:, lanes] = block
            weighted = weighted + block * w_qkv[:, lanes].astype(jnp.float32)
        elif column < 8:
            go[:, (column - 6) * UNIT : (column - 5) * UNIT] = block
        else:
            gp[:, (column - 8) * UNIT : (column - 7) * UNIT] = block
    gn[...] = jnp.sum(weighted.T, axis=0, keepdims=True) / gain[...]
    for i in range(4):
        gb[:, i * UNIT : (i + 1) * UNIT] = extras[i : i + 1, :]
        gg[:, i * UNIT : (i + 1) * UNIT] = extras[4 + i : 5 + i, :]


def unpack(reduced, extras, gain, w_qkv):
    vmem = pl.BlockSpec(memory_space=pltpu.VMEM)
    shapes = ((256, 768), (256, 256), (1, 256), (256, 512), (1, 512), (1, 512))
    return pl.pallas_call(
        unpack_kernel,
        out_shape=[jax.ShapeDtypeStruct(shape, jnp.float32) for shape in shapes],
        in_specs=[vmem] * 4,
        out_specs=[vmem] * 6,
        name="unpack",
    )(reduced, extras, gain, w_qkv)


def body(
    points, patch_ids, cell_ids, norm_gain, w_qkv, w_out, w_pool, b_pool, pool_gain, cotangent
):
    scale = 1.0 / math.sqrt(points.shape[0] * lax.axis_size("pts"))
    gain = norm_gain[None]
    cells = cell_ids.reshape(4, HALF)
    queries, keys_g, values_g, marks_f, hidden, spans = prepare(
        points, patch_ids.reshape(4, HALF), gain, w_qkv
    )
    attended, logs, sums, counts = attend(
        spans, queries, marks_f, keys_g, values_g, points, w_out, cells
    )
    dmixed, datt, deltas, gw_pool, gw_out, gb_pool, g_gain = pool(
        scale, sums, counts, cells, attended, w_out, w_pool, b_pool[None], pool_gain[None], cotangent
    )
    dq, dk, dv = attend_back(spans, queries, logs, datt, deltas, keys_g, values_g)
    grad_points, reduced, extras = finish(
        scale, hidden, dq, dk, dv, dmixed, points, gain, w_qkv, gw_out, gw_pool, gb_pool, g_gain
    )
    gq, go, gn, gp, gb, gg = unpack(reduced, extras, gain, w_qkv)
    return (grad_points, gq, go, gn[0], gp, gb[0], gg[0])


def solution(mesh):
    in_specs = (P("pts", None), P("pts"), P("pts"), P(), P(), P(), P(), P(), P(), P("pts", None))
    out_specs = (P("pts", None), P(), P(), P(), P(), P(), P())
    return jax.shard_map(body, mesh=mesh, in_specs=in_specs, out_specs=out_specs, check_vma=False)
```

time: 208 us -> 141 us (0.68)
  starting transfers between devices: 25.5 us -> 0 us
  other arithmetic: 18.1 us -> 0 us
  local copies, waits for them, and re-layouts: 19.8 us -> 8.15 us
  Pallas kernels: 122 us -> 132 us
  waiting for transfers between devices: 7.49 us -> 0 us
  between operations: 7.9 us -> 0.8 us
  matrix products: 5.82 us -> 0 us
    pallas_call x1 -> x4, Pallas kernels: 66.7 us -> 96 us  [the longest x1 61.6 us: finish(): pl.pallas_call(functools.partial(finish_kernel, scale), out_shape=[jax.Sh...]
    ppermute x8 -> x0, starting transfers between devices: 25.5 us -> none  [the longest x3 12.8 us: padded(): lax.ppermute(lax.slice_in_dim(block, block.shape[dim] - width, None, axis...]
    pallas_call x1, Pallas kernels: 35.3 us -> 21.1 us  [attend_back(): pl.pallas_call(backward_kernel, grid=(2, 2), out_shape=[jax.ShapeDtypeStr...]
    ppermute x8 -> x0, waiting for transfers between devices: 7.49 us -> none  [the longest x3 3.52 us: padded(): lax.ppermute(lax.slice_in_dim(block, 0, width, axis=dim), axis, backward)]
    reduce_sum x9 -> x0, other arithmetic: 6.2 us -> none  [the longest x1 3.28 us: key_spans(): low = jnp.sum((marks_ext[:2 * PATCH] < first).astype(jnp.int32))]
    dot_general x11 -> x0, matrix products: 5.82 us -> none  [the longest x3 2.09 us: inner_rows(): lax.dot_general(left, right, (((0,), (0,)), ((), ())), preferred_element_...]
    pallas_call x1, Pallas kernels: 20.5 us -> 14.7 us  [attend(): pl.pallas_call(forward_kernel, grid=(2, 2), out_shape=[jax.ShapeDtypeStru...]
    gather x2 -> x0, local copies, waits for them, and re-layouts: 3.46 us -> none  [body(): jnp.take(share, jnp.maximum(local_cells, 0), axis=0)]
  transfers between devices with their start and end apart: 8 -> 0, of which waited for: 3 -> 0; matrix products, arithmetic and copies ran while one was open for 7% -> 0% of each run, Pallas kernels for 0% -> 0%
where the time goes in v2:
time: 141 us
  Pallas kernels  132 us (94%)
  local copies, waits for them, and re-layouts  8.15 us (6%)
    pallas_call x1, Pallas kernels, finish(): pl.pallas_call(functools.partial(finish_kernel, scale), out_shape=[jax.Sh...  61.6 us
    pallas_call x1, Pallas kernels, attend_back(): pl.pallas_call(backward_kernel, grid=(2, 2), out_shape=[jax.ShapeDtypeStr...  21.1 us
    pallas_call x1, Pallas kernels, prepare(): pl.pallas_call(prepare_kernel, out_shape=[jax.ShapeDtypeStruct((PATCH, 25...  18.5 us
    pallas_call x1, Pallas kernels, attend(): pl.pallas_call(forward_kernel, grid=(2, 2), out_shape=[jax.ShapeDtypeStru...  14.7 us
    pallas_call x1, Pallas kernels, pool(): pl.pallas_call(functools.partial(pool_kernel, scale), out_shape=[jax.Shap...  13.3 us
    unnamed x35, local copies, waits for them, and re-layouts  8.15 us

profile of v2, /device:TPU:1, one launch (start us, length us, event | category | flops | bytes accessed | tf_op | source)
XLA Modules:
  0.0 140.7 jit_solution(17087056633384444013)
XLA Ops:
  0.6 0.0 copy-start
  0.6 1.0 copy-done
  1.6 0.0 copy-start.2
  1.6 0.9 copy-done.2
  2.6 0.0 copy-start.9
  2.6 0.7 copy-done.9
  3.3 0.0 copy-start.14
  3.3 0.7 copy-done.14
  3.9 18.5 %prepare.1 = (bf16[512,256]{1,0:T(8,128)(2,1)S(1)}, bf16[2,1536,256]{2,1,0:T(8,128)(2,1)S(1)}, bf16[2,1536,256]{2,1,0:T(8,128)(2,1)S(1)}, bf16[512,128]{1,0:T(8,...) custom-call(bf16[512,256]{1,0:T(8,128)(2,1)S(1)} %copy-done.2, s32[4,128]{1,0:T(4,128)S(1)} %bitcast.13, ...), custom_call_target="tpu_custom_call" | custom-call | tf_op jit(solution)/shard_map/prepare/pallas_call | solution.py:187
  22.5 0.0 copy-start.3
  22.5 0.9 copy-done.3
  23.4 0.0 copy-start.6
  23.4 0.9 copy-done.6
  24.3 0.0 copy-start.12
  24.3 0.7 copy-done.12
  25.0 0.0 copy-start.7
  25.0 0.0 copy-start.8
  25.0 0.0 copy-start.13
  25.0 0.0 copy-start.15
  25.0 0.0 copy-start.16
  25.0 14.7 %attention.1 = (bf16[512,256]{1,0:T(8,128)(2,1)S(1)}, bf16[512,256]{1,0:T(8,128)(2,1)S(1)}, f32[144,256]{1,0:T(8,128)S(1)}, f32[144,128]{1,0:T(8,128)S(1)}) custom-call(s32[2,2]{1,0:T(2,128)S(1)} %get-tuple-element.37.spans, bf16[512,256]{1,0:T(8,128)(2,1)S(1)} %get-tuple-element.38.q_ref, bf16[512,128]{1,0:T(8,128)(2,1)S(1)} %get-tuple-element.39.f_ref, ...), custom_call_target="tpu_custom_call" | custom-call | tf_op jit(solution)/shard_map/attention/pallas_call | solution.py:296
  39.7 0.0 copy-done.7
  39.7 0.0 copy-done.8
  39.7 0.0 copy-done.13
  39.7 0.0 copy-done.15
  39.7 0.0 copy-done.16
  39.8 13.3 %pooling.1 = (f32[512,256]{1,0:T(8,128)S(1)}, bf16[512,256]{1,0:T(8,128)(2,1)S(1)}, bf16[512,256]{1,0:T(8,128)(2,1)S(1)}, bf16[256,512]{1,0:T(8,128)(2,1)S(1)}, ...) custom-call(f32[144,256]{1,0:T(8,128)S(1)} %get-tuple-element.43.sums, ...), custom_call_target="tpu_custom_call" | custom-call | tf_op jit(solution)/shard_map/pooling/pallas_call | solution.py:413
  53.1 0.0 copy-start.1
  53.1 0.0 copy-start.4
  53.1 0.0 copy-start.10
  53.2 21.1 %attention_back.1 = (bf16[512,256]{1,0:T(8,128)(2,1)S(1)}, bf16[1536,256]{1,0:T(8,128)(2,1)S(1)}, bf16[1536,256]{1,0:T(8,128)(2,1)S(1)}) custom-call(s32[2,2]{1,0:T(2,128)S(1)} %get-tuple-element.37.spans, bf16[512,256]{1,0:T(8,128)(2,1)S(1)} %get-tuple-element.38.q_ref, bf16[512,256]{1,0:T(8,128)(2,1)S(1)} %get-tuple-element.42.logs_ref, ...), custom_call_target="tpu_custom_call" | custom-call | tf_op jit(solution)/shard_map/attention_back/pallas_call | solution.py:491
  74.2 0.0 copy-done.1
  74.2 0.0 copy-done.4
  74.3 0.0 copy-done.10
  74.3 61.6 %finish.1 = (f32[512,256]{1,0:T(8,128)S(1)}, bf16[3072,128]{1,0:T(8,128)(2,1)S(1)}, f32[16,128]{1,0:T(8,128)S(1)}) custom-call(bf16[1536,256]{1,0:T(8,128)(2,1)S(1)} %get-tuple-element.36.hidden, bf16[512,256]{1,0:T(8,128)(2,1)S(1)} %get-tuple-element.48.dq, bf16[1536,256]{1,0:T(8,128)(2,1)S(1)} %get-tuple-element.49.dk, ...), custom_call_target="tpu_custom_call" | custom-call | tf_op jit(solution)/shard_map/finish/pallas_call | solution.py:648
  135.9 0.0 copy-start.5
  135.9 0.9 copy-done.5
  136.8 0.0 copy-start.11
  136.8 0.6 copy-done.11
  137.4 2.5 %unpack.1 = (f32[256,768]{1,0:T(8,128)}, f32[256,256]{1,0:T(8,128)}, f32[1,256]{1,0:T(1,128)}, f32[256,512]{1,0:T(8,128)}, f32[1,512]{1,0:T(1,128)}, /*index=5*/f32[1,512]{1,0:T(1,128)}) custom-call(bf16[3072,128]{1,0:T(8,128)(2,1)} %copy-done.5, f32[16,128]{1,0:T(8,128)} %copy-done.11, f32[1,256]{1,0:T(1,128)} %bitcast.8, bf16[256,768]{1,0:T(8,128)(2,1)} %w_qkv.5), custom_call_target="tpu_custom_call" | custom-call | tf_op jit(solution)/shard_map/unpack/pallas_call | solution.py:699
  139.9 0.8 copy.18
Async XLA Ops:
  0.6 1.0 copy-start
  1.6 0.9 copy-start.2
  2.6 0.7 copy-start.9
  3.3 0.7 copy-start.14
  22.5 1.0 copy-start.3
  23.4 0.9 copy-start.6
  24.3 0.7 copy-start.12
  25.0 14.7 %copy-start.7 = (bf16[256,512]{1,0:T(8,128)(2,1)S(1)}, bf16[256,512]{1,0:T(8,128)(2,1)}, u32[]{:S(2)}) copy-start(bf16[256,512]{1,0:T(8,128)(2,1)} %w_pool.1) | copy-start | bytes 786436
  25.0 14.7 %copy-start.8 = (f32[128,512]{1,0:T(8,128)S(1)}, f32[128,512]{1,0:T(8,128)}, u32[]{:S(2)}) copy-start(f32[128,512]{1,0:T(8,128)} %cotangent.1) | copy-start | bytes 786436
  25.0 14.7 %copy-start.13 = (s32[512]{0:T(512)S(1)}, s32[512]{0:T(512)}, u32[]{:S(2)}) copy-start(s32[512]{0:T(512)} %param.12) | copy-start | bytes 6148
  25.0 14.7 %copy-start.15 = (f32[512]{0:T(512)S(1)}, f32[512]{0:T(512)}, u32[]{:S(2)}) copy-start(f32[512]{0:T(512)} %param.17) | copy-start | bytes 6148
  25.0 14.7 %copy-start.16 = (f32[512]{0:T(512)S(1)}, f32[512]{0:T(512)}, u32[]{:S(2)}) copy-start(f32[512]{0:T(512)} %param.18) | copy-start | bytes 6148
  53.1 21.1 %copy-start.1 = (bf16[256,768]{1,0:T(8,128)(2,1)S(1)}, bf16[256,768]{1,0:T(8,128)(2,1)}, u32[]{:S(2)}) copy-start(bf16[256,768]{1,0:T(8,128)(2,1)} %w_qkv.5) | copy-start | bytes 1179652
  53.1 21.1 %copy-start.4 = (bf16[512,256]{1,0:T(8,128)(2,1)S(1)}, bf16[512,256]{1,0:T(8,128)(2,1)}, u32[]{:S(2)}) copy-start(bf16[512,256]{1,0:T(8,128)(2,1)} %points.3) | copy-start | bytes 786436
  53.1 21.1 %copy-start.10 = (f32[256]{0:T(256)S(1)}, f32[256]{0:T(256)}, u32[]{:S(2)}) copy-start(f32[256]{0:T(256)} %param.13) | copy-start | bytes 3076
  135.9 0.9 copy-start.5
  136.8 0.6 copy-start.11
